TPU v7x, 768 devices: a whole 4x8x12 slice. The times are simulated.
768 devices in a mesh: col: 64 (over y, x, core), row: 12 (over z).
Axes of the slice: x: 4, y: 8, z: 12, core: 2. Of those that a mesh axis runs over, the one named last changes fastest.
Arguments:
- features: bfloat16 [196608, 512], P(('col', 'row')), may hold values from -6 to 6
- pick: int32 [768, 256], P(('col', 'row')), may hold values from 0 to 255, each once within a row
- tiles: bfloat16 [768, 12, 256, 256], P(('col', 'row')), may hold values from -0.109375 to 0.109375
- coords: int32 [768, 12, 2], P(('col', 'row')), may hold values from 0 to 11, as said below
- counts: int32 [768], P(('col', 'row')), may hold values from 1 to 12, as said below
- weight: bfloat16 [512, 512], replicated, may hold values from -0.25 to 0.25
- bias: float32 [512], replicated, may hold values from -3 to 3
- cotangent: bfloat16 [196608, 512], P(('col', 'row')), may hold values from -0.0134887695 to 0.0134887695
Outputs:
- hidden: bfloat16 [196608, 512], P(('col', 'row'))
- weight_grad: float32 [512, 512], replicated
- bias_grad: float32 [512], replicated
Inputs may be any that keep to these rules, and one draw needn't show every extreme that they name: `coords`: entry 0 of slot t is (t + k) mod 12 for a number k of each device; entry 1 is any block of the column. `counts`: all 12 devices of one column hold 12 live tiles.
All inputs are finite; a program needn't handle non-finite values.
Results may differ from a plain program's by a relative error of at most 0.0075.
Values may be sent and summed in bfloat16 or wider, within the bound.
No kernel may reach another device: no remote copies, remote signals or barrier semaphores. Data moves between devices by JAX's collectives and lax.ppermute only.
A program may use at most 64 MiB of HBM per device.

v0:
```python
import jax
import jax.numpy as jnp
from jax import lax
from jax.sharding import PartitionSpec as P


def on_device(features, pick, tiles, coords, counts, weight, bias, cotangent):
    col_count = lax.axis_size("col")
    row_count = lax.axis_size("row")
    block_rows = features.shape[0]
    width = features.shape[1]
    slot_rows = block_rows // col_count
    sent = features[pick[0]].reshape(col_count, slot_rows, width)
    blocked = lax.all_to_all(sent, "col", split_axis=0, concat_axis=0, tiled=True).reshape(
        block_rows, width
    )
    whole = lax.all_gather(blocked, "row", axis=0, tiled=True)
    column_blocks = whole.reshape(row_count, block_rows, width)
    tile_set = tiles[0]
    tile_max = tile_set.shape[0]
    out_index = coords[0, :, 0]
    in_index = coords[0, :, 1]
    live_count = counts[0]
    inputs = column_blocks[in_index]
    products = jnp.einsum("tab,tbf->taf", tile_set, inputs, preferred_element_type=jnp.float32)
    owners = jnp.arange(row_count, dtype=jnp.int32)
    live = jnp.arange(tile_max, dtype=jnp.int32) < live_count
    select = ((out_index[:, None] == owners) & live[:, None]).astype(jnp.float32)
    partial_value = jnp.einsum("to,taf->oaf", select, products, precision=lax.Precision.HIGHEST)
    summed = lax.psum_scatter(
        partial_value.reshape(row_count * block_rows, width), "row", scatter_dimension=0, tiled=True
    )
    aggregated = summed.astype(jnp.bfloat16)
    pre = jnp.dot(aggregated, weight, preferred_element_type=jnp.float32) + bias
    sigmoid_v = jax.nn.sigmoid(pre)
    hidden = (pre * sigmoid_v).astype(jnp.bfloat16)
    grad_pre = (cotangent.astype(jnp.float32) * sigmoid_v * (1.0 + pre * (1.0 - sigmoid_v))).astype(
        jnp.bfloat16
    )
    local_weight = jnp.dot(aggregated.T, grad_pre, preferred_element_type=jnp.float32)
    local_bias = jnp.sum(grad_pre.astype(jnp.float32), axis=0)
    weight_grad, bias_grad = lax.psum((local_weight, local_bias), ("col", "row"))
    return (hidden, weight_grad, bias_grad)


def solution(mesh):
    in_specs = (
        P(("col", "row"), None),
        P(("col", "row"), None),
        P(("col", "row"), None, None, None),
        P(("col", "row"), None, None),
        P(("col", "row")),
        P(),
        P(),
        P(("col", "row"), None),
    )
    out_specs = (P(("col", "row"), None), P(), P())
    return jax.shard_map(
        on_device, mesh=mesh, in_specs=in_specs, out_specs=out_specs, check_vma=False
    )
```

profile of v0, /device:TPU:1, one launch (start us, length us, event | category | flops | bytes accessed | tf_op | source)
XLA Modules:
  0.0 704.1 jit_solution(16251744325943100261)
XLA Ops:
  7.2 0.0 copy-start
  7.2 0.0 copy-start.5
  7.2 0.0 all-gather.2.cloned.1.call-start
  7.2 0.8 compare_select_fusion
  8.0 2.2 gather_fusion
  10.2 0.1 reshape.80
  10.3 27.0 %all_to_all.5 = bf16[64,4,512]{2,1,0:T(4,128)(2,1)S(1)} all-to-all(bf16[64,4,512]{2,1,0:T(4,128)(2,1)S(1)} %reshape.80), channel_id=1, replica_groups=mesh['col'=64,'row'=12] {'col'}, dimensions={0} | all-to-all | bytes 524288 | tf_op jit(solution)/shard_map/all_to_all | solution.py:14
  37.3 0.8 reshape.81
  38.1 0.0 all-gather.2.cloned.1.call-update
  38.1 0.0 reduce-scatter.2.cloned.1.call-start
  38.8 0.0 copy-done.5
  38.9 55.8 %all-gather.2.cloned.1.call-done = bf16[3072,512]{1,0:T(8,128)(2,1)} async-done(((bf16[256,512]{1,0:T(8,128)(2,1)}), bf16[3072,512]{1,0:T(8,128)(2,1)}) %all-gather.2.cloned.1.call-update) | async-done | bytes 3145744 | tf_op jit(solution)/shard_map/all_gather | solution.py:17
  94.7 4.4 gather_fusion.1
  99.0 0.0 copy-done
  99.0 5.7 fusion.2
  104.7 9.7 %copy.12 = f32[12,512,256]{1,0,2:T(8,128)} copy(f32[12,512,256]{2,1,0:T(8,128)} %fusion.2) | data formatting | bytes 12582912 | tf_op jit(solution)/shard_map/tab,tbf->taf/dot_general | solution.py:25
  114.5 12.7 %fusion = f32[12,256,512]{2,0,1:T(8,128)S(1)} fusion(f32[12,512,256]{1,0,2:T(8,128)} %copy.12, s32[12]{0:T(128)S(1)} %slice_bitcast_fusion, pred[12]{0:T(512)(128)(4,1)S(1)} %iota_compare_fusion.1), kind=kOutput, calls=%fused_computation.2 | convolution fusion | flops 226492704 | bytes 12582972 | tf_op jit(solution)/shard_map/to,taf->oaf/dot_general | solution.py:29
  127.2 6.3 copy.11
  133.5 0.0 copy-start.2
  133.5 0.0 copy-start.3
  133.5 0.0 copy-start.4
  133.5 0.0 reduce-scatter.2.cloned.1.call-update
  133.5 0.0 all-reduce.2.cloned.1.call-start
  133.6 88.3 %reduce-scatter.2.cloned.1.call-done = f32[256,512]{1,0:T(8,128)} async-done(((f32[3072,512]{1,0:T(8,128)}), f32[256,512]{1,0:T(8,128)}) %reduce-scatter.2.cloned.1.call-update) | async-done | bytes 524304 | tf_op jit(solution)/shard_map/reduce_scatter | solution.py:30
  221.9 0.0 copy-done.2
  221.9 0.0 copy-done.3
  221.9 0.0 copy-done.4
  221.9 0.0 copy-start.1
  221.9 2.3 convert_reduce_fusion
  224.2 0.0 copy-done.1
  224.2 1.3 fusion.4
  225.5 0.0 all-reduce.2.cloned.1.call-update
  225.5 108.1 %psum.15 = f32[512]{0:T(512)} all-reduce(f32[512]{0:T(512)S(1)} %get-tuple-element.3), channel_id=1, replica_groups=mesh['col'=64,'row'=12] {'col','row'}, use_global_device_ids=true, to_apply=%region_3.0 | all-reduce | flops 512 | bytes 4096 | tf_op jit(solution)/shard_map/psum | solution.py:42
  333.6 361.7 %all-reduce.2.cloned.1.call-done = f32[512,512]{1,0:T(8,128)} async-done(((f32[512,512]{1,0:T(8,128)}), f32[512,512]{1,0:T(8,128)}) %all-reduce.2.cloned.1.call-update) | async-done | bytes 1048592 | tf_op jit(solution)/shard_map/psum | solution.py:42
  695.3 2.3 copy.15
  (5 shorter events, 0.0 us)
Async XLA Ops:
  7.2 91.9 %copy-start = (bf16[1,12,256,256]{3,2,1,0:T(8,128)(2,1)S(1)}, bf16[1,12,256,256]{3,2,1,0:T(8,128)(2,1)}, u32[]{:S(2)}) copy-start(bf16[1,12,256,256]{3,2,1,0:T(8,128)(2,1)} %param.10) | copy-start | bytes 4718596
  7.2 31.6 %copy-start.5 = (s32[1,12,2]{1,2,0:T(2,128)S(1)}, s32[1,12,2]{1,2,0:T(2,128)}, u32[]{:S(2)}) copy-start(s32[1,12,2]{1,2,0:T(2,128)} %param.11) | copy-start | bytes 292
  7.2 87.5 %all-gather.2.cloned.1.call-start = ((), (), s32[]{:S(2)}) async-start(), calls=%async_computation.2 | async-start | bytes 3407872 | tf_op jit(solution)/shard_map/all_gather | solution.py:17
  38.1 183.8 %reduce-scatter.2.cloned.1.call-start = ((), (), s32[]{:S(2)}) async-start(), calls=%async_computation.3 | async-start | bytes 6815744 | tf_op jit(solution)/shard_map/reduce_scatter | solution.py:30
  133.5 88.4 %copy-start.2 = (bf16[512,512]{1,0:T(8,128)(2,1)S(1)}, bf16[512,512]{1,0:T(8,128)(2,1)}, u32[]{:S(2)}) copy-start(bf16[512,512]{1,0:T(8,128)(2,1)} %param.13) | copy-start | bytes 1572868
  133.5 88.4 %copy-start.3 = (bf16[256,512]{1,0:T(8,128)(2,1)S(1)}, bf16[256,512]{1,0:T(8,128)(2,1)}, u32[]{:S(2)}) copy-start(bf16[256,512]{1,0:T(8,128)(2,1)} %param.15) | copy-start | bytes 786436
  133.5 88.4 %copy-start.4 = (f32[512]{0:T(512)S(1)}, f32[512]{0:T(512)}, u32[]{:S(2)}) copy-start(f32[512]{0:T(512)} %param.14) | copy-start | bytes 6148
  133.5 561.7 %all-reduce.2.cloned.1.call-start = ((), (), s32[]{:S(2)}) async-start(), calls=%async_computation.4 | async-start | bytes 2097152 | tf_op jit(solution)/shard_map/psum | solution.py:42
  221.9 2.3 copy-start.1
Sparse Core Ops, SparseCore 0:
  38.2 56.3 all-gather.1
  133.6 88.1 reduce-scatter.1
  227.9 467.3 all-reduce.1
where the time goes:
time: 706 us; the launch traced here: 704 us
  waiting for transfers between devices  506 us (72%)
  blocking collectives  135 us (19%)
  local copies, waits for them, and re-layouts  25.7 us (4%)
  matrix products  22 us (3%)
  between operations  14.5 us (2%)
    psum x1, waiting for transfers between devices, on_device(): lax.psum((local_weight, local_bias), ('col', 'row'))  362 us
    psum x1, blocking collectives, on_device(): lax.psum((local_weight, local_bias), ('col', 'row'))  108 us
    reduce_scatter x1, waiting for transfers between devices, on_device(): lax.psum_scatter(partial_value.reshape(row_count * block_rows, width), 'r...  88.3 us
    all_gather x1, waiting for transfers between devices, on_device(): whole = lax.all_gather(blocked, 'row', axis=0, tiled=True)  55.8 us
    all_to_all x1, blocking collectives, on_device(): lax.all_to_all(sent, 'col', split_axis=0, concat_axis=0, tiled=True)  27 us
  transfers between devices with their start and end apart: 3, of which 3 were waited for; matrix products, arithmetic and copies ran while one was open for 0% of the time, Pallas kernels for 0%

commit v1 on v0

v1 whole, which is shorter than its diff:
```python
import functools

import jax
import jax.numpy as jnp
from jax import lax
from jax.experimental import pallas as pl
from jax.experimental.pallas import tpu as pltpu
from jax.sharding import PartitionSpec as P

BF16 = jnp.bfloat16
F32 = jnp.float32
LANES = 128
META_ROWS = 8
VMEM_LIMIT = 40 * 1024 * 1024
IN_VMEM = pl.BlockSpec(memory_space=pltpu.VMEM)
IN_SMEM = pl.BlockSpec(memory_space=pltpu.SMEM)
IN_PLACE = pl.BlockSpec(memory_space=pl.ANY)
PARAMS = pltpu.CompilerParams(vmem_limit_bytes=VMEM_LIMIT)


def order_tiles(first, tile_set):
    n = tile_set.shape[0]

    def kernel(first_ref, tiles_ref, out_ref, sems):
        copies = []
        for o in range(n):
            slot = lax.rem(o + n - first_ref[0], n)
            copies.append(pltpu.make_async_copy(tiles_ref.at[slot], out_ref.at[o], sems.at[o]))
            copies[-1].start()
        for copy in copies:
            copy.wait()

    return pl.pallas_call(
        kernel,
        out_shape=jax.ShapeDtypeStruct(tile_set.shape, tile_set.dtype),
        in_specs=[IN_SMEM, IN_PLACE],
        out_specs=IN_PLACE,
        scratch_shapes=[pltpu.SemaphoreType.DMA((n,))],
        compiler_params=PARAMS,
        cost_estimate=pl.CostEstimate(
            flops=0, bytes_accessed=2 * tile_set.size * 2, transcendentals=0
        ),
    )(first, tile_set)


def layer(which, tiles, blocks, weight, bias, cotangent):
    n, rows, _ = tiles.shape
    width = weight.shape[0]

    def kernel(which_ref, tiles_ref, blocks_ref, weight_ref, bias_ref, cot_ref, hidden_ref, grad_ref):
        total = jnp.zeros((rows, width), F32)
        for s in range(n):
            index = which_ref[s]
            live = (index >= 0).astype(F32).astype(BF16)
            block = blocks_ref[jnp.maximum(index, 0), :rows, :]
            total = total + jnp.dot(tiles_ref[s] * live, block, preferred_element_type=F32)
        aggregated = total.astype(BF16)
        pre = jnp.dot(aggregated, weight_ref[...], preferred_element_type=F32) + bias_ref[...]
        sig = jax.nn.sigmoid(pre)
        hidden_ref[...] = (pre * sig).astype(BF16)
        grad_pre = (cot_ref[...].astype(F32) * sig * (1.0 + pre * (1.0 - sig))).astype(BF16)
        over_nodes = (((0,), (0,)), ((), ()))
        grad_ref[:, :width] = lax.dot_general(
            aggregated, grad_pre, over_nodes, preferred_element_type=F32
        ).astype(BF16)
        ones = jnp.ones((rows, LANES), BF16)
        column = lax.dot_general(grad_pre, ones, over_nodes, preferred_element_type=F32)
        high = column.astype(BF16)
        low = (column - high.astype(F32)).astype(BF16)
        lane = lax.broadcasted_iota(jnp.int32, column.shape, 1)
        grad_ref[:, width:] = jnp.where(lane < LANES // 2, high.astype(F32), low.astype(F32)).astype(BF16)

    return pl.pallas_call(
        kernel,
        out_shape=(
            jax.ShapeDtypeStruct((rows, width), BF16),
            jax.ShapeDtypeStruct((width, width + LANES), BF16),
        ),
        in_specs=[IN_SMEM] + [IN_VMEM] * 5,
        out_specs=(IN_VMEM, IN_VMEM),
        compiler_params=PARAMS,
        cost_estimate=pl.CostEstimate(
            flops=2 * rows * width * (n * rows + 2 * width),
            bytes_accessed=6 * 1024 * 1024,
            transcendentals=rows * width,
        ),
    )(which, tiles, blocks, weight, bias, cotangent)


def sum_over_col(parts, copies):
    n, rows, wide = parts.shape

    def kernel(parts_ref, out_ref):
        total = parts_ref[0].astype(F32)
        for i in range(1, n):
            total = total + parts_ref[i].astype(F32)
        for i in range(copies):
            out_ref[i] = total

    return pl.pallas_call(
        kernel,
        out_shape=jax.ShapeDtypeStruct((copies, rows, wide), F32),
        in_specs=[IN_VMEM],
        out_specs=IN_VMEM,
        compiler_params=PARAMS,
    )(parts)


def sum_over_row(place, parts, copies, width):
    n, rows, wide = parts.shape

    def kernel(place_ref, parts_ref, out_ref):
        total = parts_ref[0]
        for i in range(1, n):
            total = total + parts_ref[i]
        column = total[:, width : width + 1] + total[:, width + LANES // 2 : width + LANES // 2 + 1]
        lane = lax.broadcasted_iota(jnp.int32, (rows, LANES), 1)
        row = lax.broadcasted_iota(jnp.int32, (rows, LANES), 0)
        mine = lane == lax.rem(place_ref[0] * rows, LANES) + row
        line = jnp.sum(jnp.where(mine, column, 0.0), axis=0, keepdims=True)
        high = line.astype(BF16).astype(F32)
        tail = jnp.where(row == 0, high, jnp.where(row == 1, line - high, 0.0)).astype(BF16)
        weights = total[:, :width].astype(BF16)
        for i in range(copies):
            out_ref[i, :, :width] = weights
            out_ref[i, :, width:] = tail

    return pl.pallas_call(
        kernel,
        out_shape=jax.ShapeDtypeStruct((copies, rows, wide), BF16),
        in_specs=[IN_SMEM, IN_VMEM],
        out_specs=IN_VMEM,
        compiler_params=PARAMS,
    )(place, parts)


def unpack(parts, width):
    n, rows, wide = parts.shape
    per_group = LANES // rows

    def kernel(parts_ref, weight_ref, bias_ref):
        for i in range(n):
            weight_ref[i * rows : (i + 1) * rows, :] = parts_ref[i, :, :width].astype(F32)
        for g in range(n // per_group):
            line = parts_ref[g * per_group, :, width:].astype(F32)
            for i in range(1, per_group):
                line = line + parts_ref[g * per_group + i, :, width:].astype(F32)
            bias_ref[:, g * LANES : (g + 1) * LANES] = jnp.sum(line, axis=0, keepdims=True)

    return pl.pallas_call(
        kernel,
        out_shape=(
            jax.ShapeDtypeStruct((n * rows, width), F32),
            jax.ShapeDtypeStruct((1, n * rows), F32),
        ),
        in_specs=[IN_VMEM],
        out_specs=(IN_VMEM, IN_VMEM),
        compiler_params=PARAMS,
    )(parts)


def on_device(features, pick, tiles, coords, counts, weight, bias, cotangent):
    col_count = lax.axis_size("col")
    row_count = lax.axis_size("row")
    block_rows, width = features.shape
    slot_rows = block_rows // col_count
    exchange = functools.partial(lax.all_to_all, split_axis=0, concat_axis=0, tiled=True)

    sent = features[pick[0]].reshape(col_count, slot_rows, width)
    blocked = exchange(sent, "col").reshape(block_rows, width)

    first = coords[0, :1, 0]
    slots = lax.rem(jnp.arange(row_count, dtype=jnp.int32) + row_count - first, row_count)
    inputs = jnp.where(slots < counts[0], coords[0, slots, 1], -1)
    meta = jnp.zeros((META_ROWS, width), BF16).at[0, :row_count].set(inputs.astype(BF16))
    whole = lax.all_gather(jnp.concatenate([blocked, meta], axis=0), "row", axis=0, tiled=True)
    whole = whole.reshape(row_count, block_rows + META_ROWS, width)

    ordered = order_tiles(first, tiles[0])
    ordered, _ = lax.optimization_barrier((ordered, blocked))
    mine = exchange(ordered, "row")

    me = lax.axis_index("row")
    which = lax.dynamic_index_in_dim(whole[:, block_rows, :row_count], me, 1, keepdims=False)
    hidden, grads = layer(
        which.astype(jnp.int32), mine, whole, weight, bias.reshape(1, width), cotangent
    )

    grad_rows = width // col_count
    parts = exchange(grads.reshape(col_count, grad_rows, width + LANES), "col")
    parts = exchange(sum_over_col(parts, row_count), "row")
    place = lax.axis_index("col").astype(jnp.int32).reshape(1)
    parts = exchange(sum_over_row(place, parts, col_count, width), "col")
    weight_grad, bias_grad = unpack(parts, width)
    return hidden, weight_grad, bias_grad.reshape(width)


def solution(mesh):
    in_specs = (
        P(("col", "row"), None),
        P(("col", "row"), None),
        P(("col", "row"), None, None, None),
        P(("col", "row"), None, None),
        P(("col", "row")),
        P(),
        P(),
        P(("col", "row"), None),
    )
    out_specs = (P(("col", "row"), None), P(), P())
    return jax.shard_map(
        on_device, mesh=mesh, in_specs=in_specs, out_specs=out_specs, check_vma=False
    )
```

time: 706 us -> 234 us (0.33)
  waiting for transfers between devices: 506 us -> 114 us
  blocking collectives: 135 us -> 56.3 us
  starting transfers between devices: 0.12 us -> 32.5 us
  matrix products: 22 us -> 0 us
  local copies, waits for them, and re-layouts: 25.7 us -> 6.15 us
    psum x1 -> x0, waiting for transfers between devices: 362 us -> none  [on_device(): lax.psum((local_weight, local_bias), ('col', 'row'))]
    psum x1 -> x0, blocking collectives: 108 us -> none  [on_device(): lax.psum((local_weight, local_bias), ('col', 'row'))]
    reduce_scatter x1 -> x0, waiting for transfers between devices: 88.3 us -> none  [on_device(): lax.psum_scatter(partial_value.reshape(row_count * block_rows, width), 'r...]
    all_gather x1, waiting for transfers between devices: 55.8 us -> 90.6 us  [on_device(): lax.all_gather(jnp.concatenate([blocked, meta], axis=0), 'row', axis=0, t...]
    all_to_all x0 -> x3, starting transfers between devices: none -> 32.4 us  [the longest x1 14.6 us: on_device(): blocked = exchange(sent, 'col').reshape(block_rows, width)]
    all_to_all x1 -> x2, blocking collectives: 27 us -> 56.3 us  [the longest x1 28.2 us: on_device(): parts = exchange(sum_over_row(place, parts, col_count, width), 'col')]
    all_to_all x0 -> x3, waiting for transfers between devices: none -> 23.3 us  [the longest x1 13.3 us: on_device(): parts = exchange(sum_over_col(parts, row_count), 'row')]
    dot_general x4 -> x0, matrix products: 22 us -> none  [the longest x1 12.7 us: on_device(): jnp.einsum('to,taf->oaf', select, products, precision=lax.Precision.HIGHEST)]
  transfers between devices with their start and end apart: 3 -> 4, of which waited for: 3 -> 3; matrix products, arithmetic and copies ran while one was open for 0% -> 2% of each run, Pallas kernels for 0% -> 1%
where the time goes in v1:
time: 234 us; the launch traced here: 233 us
  waiting for transfers between devices  114 us (49%)
  blocking collectives  56.3 us (24%)
  starting transfers between devices  32.5 us (14%)
  between operations  14.8 us (6%)
  Pallas kernels  6.52 us (3%)
  local copies, waits for them, and re-layouts  6.15 us (3%)
  other arithmetic  3.16 us (1%)
    all_gather x1, waiting for transfers between devices, on_device(): lax.all_gather(jnp.concatenate([blocked, meta], axis=0), 'row', axis=0, t...  90.6 us
    all_to_all x1, blocking collectives, on_device(): parts = exchange(sum_over_row(place, parts, col_count, width), 'col')  28.2 us
    all_to_all x1, blocking collectives, on_device(): parts = exchange(grads.reshape(col_count, grad_rows, width + LANES), 'col')  28.1 us
    all_to_all x1, starting transfers between devices, on_device(): blocked = exchange(sent, 'col').reshape(block_rows, width)  14.6 us
    all_to_all x1, waiting for transfers between devices, on_device(): parts = exchange(sum_over_col(parts, row_count), 'row')  13.3 us
    all_to_all x1, starting transfers between devices, on_device(): mine = exchange(ordered, 'row')  12 us
    all_to_all x1, waiting for transfers between devices, on_device(): blocked = exchange(sent, 'col').reshape(block_rows, width)  9.97 us
    all_to_all x1, starting transfers between devices, on_device(): parts = exchange(sum_over_col(parts, row_count), 'row')  5.9 us
  transfers between devices with their start and end apart: 4, of which 3 were waited for; matrix products, arithmetic and copies ran while one was open for 2% of the time, Pallas kernels for 1%

profile of v1, /device:TPU:1, one launch (start us, length us, event | category | flops | bytes accessed | tf_op | source)
XLA Modules:
  0.0 233.3 jit_solution(17366657160102496509)
XLA Ops:
  7.2 0.0 copy-start
  7.2 0.7 compare_select_fusion
  7.9 0.2 copy-done
  8.1 0.0 copy-start.6
  8.1 1.2 gather_fusion
  9.3 0.0 copy-start.2
  9.3 0.8 reshape.128
  10.1 14.6 %all-to-all-start = ((bf16[64,4,512]{2,1,0:T(4,128)(2,1)}), bf16[64,4,512]{2,1,0:T(4,128)(2,1)S(1)}, u32[]{:S(2)}, u32[]{:S(2)}) async-start(bf16[64,4,512]{2,1,0:T(4,128)(2,1)} %reshape.128), calls=%async_computation | async-start | bytes 524288 | tf_op jit(solution)/shard_map/all_to_all | solution.py:170
  24.7 0.0 all-gather.2.cloned.1.call-start
  25.3 0.0 copy-done.6
  25.4 0.5 slice.22
  25.9 0.7 fusion.6
  26.5 0.7 gather_fusion.1
  27.3 0.7 fusion.2
  27.9 10.0 %all-to-all-done = bf16[64,4,512]{2,1,0:T(4,128)(2,1)S(1)} async-done(((bf16[64,4,512]{2,1,0:T(4,128)(2,1)}), bf16[64,4,512]{2,1,0:T(4,128)(2,1)S(1)}, u32[]{:S(2)}, u32[]{:S(2)}) %all-to-all-start) | async-done | bytes 262176 | tf_op jit(solution)/shard_map/all_to_all | solution.py:170
  37.9 0.1 reshape.129
  38.0 0.7 fusion.1
  38.7 0.0 all-gather.2.cloned.1.call-update
  38.7 0.0 copy-done.2
  38.7 1.9 shard_map.103
  40.7 0.0 copy-start.3
  40.7 0.0 copy-start.4
  40.7 0.0 copy-start.5
  40.7 12.0 %all-to-all-start.1 = ((bf16[12,256,256]{2,1,0:T(8,128)(2,1)}), bf16[12,256,256]{2,1,0:T(8,128)(2,1)S(1)}, u32[]{:S(2)}, u32[]{:S(2)}) async-start(bf16[12,256,256]{2,1,0:T(8,128)(2,1)} %shard_map.103), calls=%async_computation.1 | async-start | bytes 3145728 | tf_op jit(solution)/shard_map/all_to_all | solution.py:181
  52.7 90.6 %all-gather.2.cloned.1.call-done = bf16[3168,512]{1,0:T(8,128)(2,1)} async-done(((bf16[264,512]{1,0:T(8,128)(2,1)}), bf16[3168,512]{1,0:T(8,128)(2,1)}) %all-gather.2.cloned.1.call-update) | async-done | bytes 3244048 | tf_op jit(solution)/shard_map/all_gather | solution.py:176
  143.3 0.7 slice.29
  144.0 0.4 convert_reduce_fusion.which_ref
  144.4 0.0 all-to-all-done.1.tiles_ref
  144.4 0.0 copy-done.3
  144.4 0.0 copy-done.4
  144.4 0.0 copy-done.5
  144.4 0.0 copy-start.1
  144.4 1.9 copy-done.1
  146.3 2.6 %shard_map.104 = (bf16[256,512]{1,0:T(8,128)(2,1)}, bf16[512,640]{1,0:T(8,128)(2,1)S(1)}) custom-call(s32[12]{0:T(128)S(1)} %convert_reduce_fusion.which_ref, bf16[12,256,256]{2,1,0:T(8,128)(2,1)S(1)} %all-to-all-done.1.tiles_ref, bf16[12,264,512]{2,1,0:T(8,128)(2,1)S(1)} %bitcast.18, bf16[512,512]{1,0:T(8,128)(2,1)S(1)} %copy-done.3, ...), custom_call_target="tpu_custom_call" | custom-call | flops 1073741824 | bytes 6291456 | tf_op jit(solution)/shard_map/pallas_call | solution.py:73
  148.9 28.1 %all_to_all.25.parts_ref = bf16[64,8,640]{2,1,0:T(8,128)(2,1)S(1)} all-to-all(bf16[64,8,640]{2,1,0:T(8,128)(2,1)S(1)} %bitcast.20), channel_id=1, replica_groups=mesh['col'=64,'row'=12] {'col'}, dimensions={0} | all-to-all | bytes 1310720 | tf_op jit(solution)/shard_map/all_to_all | solution.py:190
  177.0 0.8 shard_map.105
  177.8 5.9 %all-to-all-start.3 = ((f32[12,8,640]{2,1,0:T(8,128)}), f32[12,8,640]{2,1,0:T(8,128)S(1)}, u32[]{:S(2)}, u32[]{:S(2)}) async-start(f32[12,8,640]{2,1,0:T(8,128)} %shard_map.105), calls=%async_computation.3 | async-start | bytes 491520 | tf_op jit(solution)/shard_map/all_to_all | solution.py:191
  183.7 13.3 %all-to-all-done.3.parts_ref = f32[12,8,640]{2,1,0:T(8,128)S(1)} async-done(((f32[12,8,640]{2,1,0:T(8,128)}), f32[12,8,640]{2,1,0:T(8,128)S(1)}, u32[]{:S(2)}, u32[]{:S(2)}) %all-to-all-start.3) | async-done | bytes 245792 | tf_op jit(solution)/shard_map/all_to_all | solution.py:191
  197.1 0.2 shard_map.106
  197.2 28.2 %all_to_all.26.parts_ref = bf16[64,8,640]{2,1,0:T(8,128)(2,1)S(1)} all-to-all(bf16[64,8,640]{2,1,0:T(8,128)(2,1)S(1)} %shard_map.106), channel_id=1, replica_groups=mesh['col'=64,'row'=12] {'col'}, dimensions={0} | all-to-all | bytes 1310720 | tf_op jit(solution)/shard_map/all_to_all | solution.py:193
  225.4 1.0 shard_map.107
  (1 shorter events, 0.0 us)
Async XLA Ops:
  7.2 1.0 copy-start
  8.1 17.2 %copy-start.6 = (s32[1,12,2]{1,2,0:T(2,128)S(1)}, s32[1,12,2]{1,2,0:T(2,128)}, u32[]{:S(2)}) copy-start(s32[1,12,2]{1,2,0:T(2,128)} %param.13) | copy-start | bytes 292
  9.3 29.4 %copy-start.2 = (bf16[1,12,256,256]{3,2,1,0:T(8,128)(2,1)S(1)}, bf16[1,12,256,256]{3,2,1,0:T(8,128)(2,1)}, u32[]{:S(2)}) copy-start(bf16[1,12,256,256]{3,2,1,0:T(8,128)(2,1)} %param.12) | copy-start | bytes 4718596
  10.1 27.8 %all-to-all-start = ((bf16[64,4,512]{2,1,0:T(4,128)(2,1)}), bf16[64,4,512]{2,1,0:T(4,128)(2,1)S(1)}, u32[]{:S(2)}, u32[]{:S(2)}) async-start(bf16[64,4,512]{2,1,0:T(4,128)(2,1)} %reshape.128), calls=%async_computation | async-start | bytes 524288 | tf_op jit(solution)/shard_map/all_to_all | solution.py:170
  24.7 118.6 %all-gather.2.cloned.1.call-start = ((), (), s32[]{:S(2)}) async-start(), calls=%async_computation.5 | async-start | bytes 3514368 | tf_op jit(solution)/shard_map/all_gather | solution.py:176
  40.7 103.7 %copy-start.3 = (bf16[512,512]{1,0:T(8,128)(2,1)S(1)}, bf16[512,512]{1,0:T(8,128)(2,1)}, u32[]{:S(2)}) copy-start(bf16[512,512]{1,0:T(8,128)(2,1)} %weight_ref.1) | copy-start | bytes 1572868
  40.7 103.7 %copy-start.4 = (bf16[256,512]{1,0:T(8,128)(2,1)S(1)}, bf16[256,512]{1,0:T(8,128)(2,1)}, u32[]{:S(2)}) copy-start(bf16[256,512]{1,0:T(8,128)(2,1)} %cot_ref.1) | copy-start | bytes 786436
  40.7 103.7 %copy-start.5 = (f32[512]{0:T(512)S(1)}, f32[512]{0:T(512)}, u32[]{:S(2)}) copy-start(f32[512]{0:T(512)} %param.16) | copy-start | bytes 6148
  40.7 103.7 %all-to-all-start.1 = ((bf16[12,256,256]{2,1,0:T(8,128)(2,1)}), bf16[12,256,256]{2,1,0:T(8,128)(2,1)S(1)}, u32[]{:S(2)}, u32[]{:S(2)}) async-start(bf16[12,256,256]{2,1,0:T(8,128)(2,1)} %shard_map.103), calls=%async_computation.1 | async-start | bytes 3145728 | tf_op jit(solution)/shard_map/all_to_all | solution.py:181
  144.4 1.9 copy-start.1
  177.8 19.2 %all-to-all-start.3 = ((f32[12,8,640]{2,1,0:T(8,128)}), f32[12,8,640]{2,1,0:T(8,128)S(1)}, u32[]{:S(2)}, u32[]{:S(2)}) async-start(f32[12,8,640]{2,1,0:T(8,128)} %shard_map.105), calls=%async_computation.3 | async-start | bytes 491520 | tf_op jit(solution)/shard_map/all_to_all | solution.py:191
Sparse Core Ops, SparseCore 0:
  38.8 104.3 all-gather.1

commit v2 on v1

v2 whole, which is shorter than its diff:
```python
import functools

import jax
import jax.numpy as jnp
from jax import lax
from jax.experimental import pallas as pl
from jax.experimental.pallas import tpu as pltpu
from jax.sharding import PartitionSpec as P

BF16 = jnp.bfloat16
F32 = jnp.float32
LANES = 128
META_ROWS = 16
STRIDE = 4
STRIDE = 4
ROUTES = ((0, 0, 2), (1, 0, 2), (-1, 0, 2), (2, 0, 1), (-2, 1, 2))
VMEM_LIMIT = 16 * 1024 * 1024
IN_VMEM = pl.BlockSpec(memory_space=pltpu.VMEM)
IN_SMEM = pl.BlockSpec(memory_space=pltpu.SMEM)
IN_PLACE = pl.BlockSpec(memory_space=pl.ANY)
PARAMS = pltpu.CompilerParams(vmem_limit_bytes=VMEM_LIMIT)


def bundle_tiles(place, count, coords, tile_set):
    n, rows, columns = tile_set.shape
    size, half = n // STRIDE, rows // 2
    heights = [(last - begin) * half for _, begin, last in ROUTES]
    pieces = len(heights) * size

    def kernel(place_ref, count_ref, coords_ref, tiles_ref, *refs):
        out_refs, (meta, tile_sems, meta_sems) = refs[: len(heights)], refs[len(heights) :]
        here, turn, first = place_ref[0], place_ref[1], coords_ref[0]
        copies = []
        for g, (behind, begin, _) in enumerate(ROUTES):
            for p in range(size):
                i = g * size + p
                output = here + turn * (p * STRIDE - behind)
                slot = lax.rem(output - first + 3 * n, n)
                source = tiles_ref.at[slot, pl.ds(begin * half, heights[g])]
                target = out_refs[g].at[p, pl.ds(0, heights[g])]
                copies.append(pltpu.make_async_copy(source, target, tile_sems.at[i]))
                copies[-1].start()
                block = jnp.where(slot < count_ref[0], coords_ref[2 * slot + 1], -1)
                meta[i] = jnp.full(meta.shape[1:], block.astype(F32), F32).astype(BF16)
                note = out_refs[g].at[p, pl.ds(heights[g], META_ROWS)]
                copies.append(pltpu.make_async_copy(meta.at[i], note, meta_sems.at[i]))
                copies[-1].start()
        for copy in copies:
            copy.wait()

    return pl.pallas_call(
        kernel,
        out_shape=[
            jax.ShapeDtypeStruct((size, height + META_ROWS, columns), tile_set.dtype)
            for height in heights
        ],
        in_specs=[IN_SMEM] * 3 + [IN_PLACE],
        out_specs=[IN_PLACE] * len(heights),
        scratch_shapes=[
            pltpu.VMEM((pieces, META_ROWS, columns), tile_set.dtype),
            pltpu.SemaphoreType.DMA((pieces,)),
            pltpu.SemaphoreType.DMA((pieces,)),
        ],
        compiler_params=PARAMS,
        cost_estimate=pl.CostEstimate(
            flops=0, bytes_accessed=2 * tile_set.size * 2, transcendentals=0
        ),
    )(place, count, coords, tile_set)


def partial_sums(bundles, blocks):
    groups, size = len(bundles), bundles[0].shape[0]
    n, rows, width = blocks.shape
    half = rows // 2

    def kernel(*refs):
        bundle_refs, blocks_ref = refs[:groups], refs[groups]
        out_refs, sums = refs[groups + 1 : -1], refs[-1]
        sums[...] = jnp.zeros_like(sums)
        for p in range(size):
            for bundle_ref, (_, begin, last) in zip(bundle_refs, ROUTES):
                height = (last - begin) * half
                note = bundle_ref[p, height : height + META_ROWS, :LANES].astype(F32)
                block = jnp.max(note).astype(jnp.int32)

                @pl.when(block >= 0)
                def _():
                    sums[p, begin * half : last * half, :] += jnp.dot(
                        bundle_ref[p, :height, :], blocks_ref[block], preferred_element_type=F32
                    )

        for p, out_ref in enumerate(out_refs):
            out_ref[...] = sums[p].astype(out_ref.dtype)

    return pl.pallas_call(
        kernel,
        out_shape=[
            jax.ShapeDtypeStruct((rows, width), F32 if p == 0 else BF16) for p in range(size)
        ],
        in_specs=[IN_VMEM] * (groups + 1),
        out_specs=[IN_VMEM] * size,
        scratch_shapes=[pltpu.VMEM((size, rows, width), F32)],
        compiler_params=PARAMS,
        cost_estimate=pl.CostEstimate(
            flops=2 * n * rows * rows * width,
            bytes_accessed=6 * 1024 * 1024,
            transcendentals=0,
        ),
    )(*bundles, blocks)


def layer(core, sums, weight, bias, cotangent):
    rows, width = cotangent.shape
    parts, half = len(sums), width // 2

    def kernel(core_ref, *refs):
        sum_refs = refs[:parts]
        weight_ref, bias_ref, cot_ref, hidden_ref, keep_ref, give_ref = refs[parts:]
        total = sum_refs[0][...].astype(F32)
        for sum_ref in sum_refs[1:]:
            total = total + sum_ref[...].astype(F32)
        aggregated = total.astype(BF16)
        pre = jnp.dot(aggregated, weight_ref[...], preferred_element_type=F32) + bias_ref[...]
        sig = jax.nn.sigmoid(pre)
        hidden_ref[...] = (pre * sig).astype(BF16)
        grad_pre = (cot_ref[...].astype(F32) * sig * (1.0 + pre * (1.0 - sig))).astype(BF16)
        over_nodes = (((0,), (0,)), ((), ()))
        ones = jnp.ones((rows, LANES), BF16)
        first = core_ref[0] == 0
        for out_ref, low in ((keep_ref, first), (give_ref, jnp.logical_not(first))):
            left = jnp.where(low, aggregated[:, :half], aggregated[:, half:])
            out_ref[:, :width] = lax.dot_general(
                left, grad_pre, over_nodes, preferred_element_type=F32
            ).astype(BF16)
            left = jnp.where(low, grad_pre[:, :half], grad_pre[:, half:])
            out_ref[:, width:] = lax.dot_general(
                left, ones, over_nodes, preferred_element_type=F32
            ).astype(BF16)

    gradient = jax.ShapeDtypeStruct((half, width + LANES), BF16)
    return pl.pallas_call(
        kernel,
        out_shape=(jax.ShapeDtypeStruct((rows, width), BF16), gradient, gradient),
        in_specs=[IN_SMEM] + [IN_VMEM] * (parts + 3),
        out_specs=(IN_VMEM, IN_VMEM, IN_VMEM),
        compiler_params=PARAMS,
        cost_estimate=pl.CostEstimate(
            flops=4 * rows * width * width,
            bytes_accessed=3 * 1024 * 1024,
            transcendentals=rows * width,
        ),
    )(core, *sums, weight, bias, cotangent)


def sum_two(left, right):
    def kernel(left_ref, right_ref, out_ref):
        out_ref[...] = (left_ref[...].astype(F32) + right_ref[...].astype(F32)).astype(BF16)

    return pl.pallas_call(
        kernel,
        out_shape=jax.ShapeDtypeStruct(left.shape, BF16),
        in_specs=[IN_VMEM] * 2,
        out_specs=IN_VMEM,
        compiler_params=PARAMS,
    )(left, right)


def sum_over_chips(parts, copies):
    n, rows, wide = parts.shape

    def kernel(parts_ref, out_ref):
        total = parts_ref[0].astype(F32)
        for i in range(1, n):
            total = total + parts_ref[i].astype(F32)
        packed = total.astype(BF16)
        for i in range(copies):
            out_ref[i] = packed

    return pl.pallas_call(
        kernel,
        out_shape=jax.ShapeDtypeStruct((copies, rows, wide), BF16),
        in_specs=[IN_VMEM],
        out_specs=IN_VMEM,
        compiler_params=PARAMS,
    )(parts)


def sum_over_row(chip, parts, copies, width):
    n, rows, wide = parts.shape

    def kernel(chip_ref, parts_ref, out_ref):
        total = parts_ref[0].astype(F32)
        for i in range(1, n):
            total = total + parts_ref[i].astype(F32)
        lane = lax.broadcasted_iota(jnp.int32, (rows, LANES), 1)
        row = lax.broadcasted_iota(jnp.int32, (rows, LANES), 0)
        mine = lane == lax.rem(chip_ref[0] * rows, LANES) + row
        tail = jnp.where(mine, total[:, width:], 0.0).astype(BF16)
        weights = total[:, :width].astype(BF16)
        for i in range(copies):
            out_ref[i, :, :width] = weights
            out_ref[i, :, width:] = tail

    return pl.pallas_call(
        kernel,
        out_shape=jax.ShapeDtypeStruct((copies, rows, wide), BF16),
        in_specs=[IN_SMEM, IN_VMEM],
        out_specs=IN_VMEM,
        compiler_params=PARAMS,
    )(chip, parts)


def unpack(core, mine, other, width):
    n, rows, wide = mine.shape
    per_group = LANES // rows
    half = n * rows

    def kernel(core_ref, mine_ref, other_ref, weight_ref, bias_ref):
        for parts_ref, at in ((mine_ref, core_ref[0]), (other_ref, 1 - core_ref[0])):
            base = pl.multiple_of(at * half, half)
            for i in range(n):
                weight_ref[pl.ds(base + i * rows, rows), :] = parts_ref[i, :, :width].astype(F32)
            for g in range(n // per_group):
                line = parts_ref[g * per_group, :, width:].astype(F32)
                for i in range(1, per_group):
                    line = line + parts_ref[g * per_group + i, :, width:].astype(F32)
                line = jnp.sum(line, axis=0, keepdims=True)
                bias_ref[:, pl.ds(pl.multiple_of(base + g * LANES, LANES), LANES)] = line

    return pl.pallas_call(
        kernel,
        out_shape=(
            jax.ShapeDtypeStruct((2 * half, width), F32),
            jax.ShapeDtypeStruct((1, 2 * half), F32),
        ),
        in_specs=[IN_SMEM, IN_VMEM, IN_VMEM],
        out_specs=(IN_VMEM, IN_VMEM),
        compiler_params=PARAMS,
    )(core, mine, other)


def on_device(features, pick, tiles, coords, counts, weight, bias, cotangent):
    col_count = lax.axis_size("col")
    row_count = lax.axis_size("row")
    block_rows, width = features.shape
    slot_rows = block_rows // col_count
    exchange = functools.partial(lax.all_to_all, split_axis=0, concat_axis=0, tiled=True)

    def permute(x, step):
        pairs = []
        for col in range(col_count):
            turn = 1 - 2 * (col % 2)
            for row in range(row_count):
                target = (row + turn * step(turn * row % row_count)) % row_count
                pairs.append((col * row_count + row, col * row_count + target))
        return lax.ppermute(x, ("col", "row"), pairs)

    col, row = (lax.axis_index(axis).astype(jnp.int32) for axis in ("col", "row"))
    place = jnp.stack([row, 1 - 2 * lax.rem(col, 2)])

    sent = features[pick[0]].reshape(col_count, slot_rows, width)
    blocked = exchange(sent, "col").reshape(block_rows, width)
    blocks = lax.all_gather(blocked, "row", axis=0)

    bundles = bundle_tiles(place, counts, coords.reshape(-1), tiles[0])
    bundles = [
        permute(x, lambda _, behind=route[0]: -behind) if route[0] else x
        for x, route in zip(bundles, ROUTES)
    ]
    sums = partial_sums(bundles, blocks)
    sums = [sums[0]] + [permute(sums[p], lambda _, p=p: p * STRIDE) for p in range(1, len(sums))]
    core = lax.rem(col, 2).reshape(1)
    hidden, keep, give = layer(core, sums, weight, bias.reshape(1, width), cotangent)

    chips = col_count // 2
    cores = [[2 * chip + k for chip in range(chips)] for k in range(2)]
    other_core = [(i, i ^ 1) for i in range(col_count)]
    parts = sum_two(keep, lax.ppermute(give, "col", other_core))
    parts = parts.reshape(chips, width // col_count, width + LANES)
    parts = exchange(parts, "col", axis_index_groups=cores)
    parts = exchange(sum_over_chips(parts, row_count), "row")
    parts = sum_over_row(lax.div(col, 2).reshape(1), parts, chips, width)
    mine = exchange(parts, "col", axis_index_groups=cores)
    other = lax.ppermute(mine, "col", other_core)
    weight_grad, bias_grad = unpack(core, mine, other, width)
    return hidden, weight_grad, bias_grad.reshape(width)


def solution(mesh):
    in_specs = (
        P(("col", "row"), None),
        P(("col", "row"), None),
        P(("col", "row"), None, None, None),
        P(("col", "row"), None, None),
        P(("col", "row")),
        P(),
        P(),
        P(("col", "row"), None),
    )
    out_specs = (P(("col", "row"), None), P(), P())
    return jax.shard_map(
        on_device, mesh=mesh, in_specs=in_specs, out_specs=out_specs, check_vma=False
    )
```

time: 234 us -> 220 us (0.940)
  waiting for transfers between devices: 114 us -> 69 us
  starting transfers between devices: 32.5 us -> 53.7 us
  blocking collectives: 56.3 us -> 66.2 us
  Pallas kernels: 6.52 us -> 10.1 us
    all_gather x1, waiting for transfers between devices: 90.6 us -> 21.7 us  [on_device(): blocks = lax.all_gather(blocked, 'row', axis=0)]
    ppermute x0 -> x8, starting transfers between devices: none -> 42.6 us  [the longest x6 30.4 us: permute(): return lax.ppermute(x, ('col', 'row'), pairs)]
    ppermute x0 -> x8, waiting for transfers between devices: none -> 36.9 us  [the longest x6 34.4 us: permute(): return lax.ppermute(x, ('col', 'row'), pairs)]
    all_to_all x3 -> x1, starting transfers between devices: 32.4 us -> 11.1 us  [on_device(): parts = exchange(sum_over_chips(parts, row_count), 'row')]
    all_to_all x3 -> x1, waiting for transfers between devices: 23.3 us -> 10.4 us  [on_device(): parts = exchange(sum_over_chips(parts, row_count), 'row')]
    all_to_all x2 -> x3, blocking collectives: 56.3 us -> 66.2 us  [the longest x1 27 us: on_device(): blocked = exchange(sent, 'col').reshape(block_rows, width)]
    pallas_call x3 -> x5, Pallas kernels: 3.78 us -> 8.61 us  [the longest x1 3.49 us: partial_sums(): pl.pallas_call(kernel, out_shape=[jax.ShapeDtypeStruct((rows, width), F32...]
  transfers between devices with their start and end apart: 4 -> 10, of which waited for: 3 -> 8; matrix products, arithmetic and copies ran while one was open for 2% -> 0% of each run, Pallas kernels for 1% -> 1%
where the time goes in v2:
time: 220 us; the launch traced here: 219 us
  waiting for transfers between devices  69 us (31%)
  blocking collectives  66.2 us (30%)
  starting transfers between devices  53.7 us (24%)
  between operations  14.8 us (7%)
  Pallas kernels  10.1 us (5%)
  local copies, waits for them, and re-layouts  4.15 us (2%)
    ppermute x6, waiting for transfers between devices, permute(): return lax.ppermute(x, ('col', 'row'), pairs)  34.4 us
    ppermute x6, starting transfers between devices, permute(): return lax.ppermute(x, ('col', 'row'), pairs)  30.4 us
    all_to_all x1, blocking collectives, on_device(): blocked = exchange(sent, 'col').reshape(block_rows, width)  27 us
    all_to_all x1, blocking collectives, on_device(): parts = exchange(parts, 'col', axis_index_groups=cores)  23.9 us
    all_gather x1, waiting for transfers between devices, on_device(): blocks = lax.all_gather(blocked, 'row', axis=0)  21.7 us
    all_to_all x1, blocking collectives, on_device(): mine = exchange(parts, 'col', axis_index_groups=cores)  15.3 us
    all_to_all x1, starting transfers between devices, on_device(): parts = exchange(sum_over_chips(parts, row_count), 'row')  11.1 us
    all_to_all x1, waiting for transfers between devices, on_device(): parts = exchange(sum_over_chips(parts, row_count), 'row')  10.4 us
  transfers between devices with their start and end apart: 10, of which 8 were waited for; matrix products, arithmetic and copies ran while one was open for 0% of the time, Pallas kernels for 1%

profile of v2, /device:TPU:1, one launch (start us, length us, event | category | flops | bytes accessed | tf_op | source)
XLA Modules:
  0.0 218.9 jit_solution(2444126831848425890)
XLA Ops:
  7.2 0.0 copy-start
  7.2 0.0 copy-start.6
  7.2 0.0 copy-start.2
  7.2 0.0 all-gather.2.cloned.1.call-start
  7.2 0.8 compare_select_fusion
  8.1 0.1 copy-done
  8.1 1.2 gather_fusion
  9.3 0.1 reshape.57
  9.3 27.0 %all_to_all.20 = bf16[64,4,512]{2,1,0:T(4,128)(2,1)S(1)} all-to-all(bf16[64,4,512]{2,1,0:T(4,128)(2,1)S(1)} %reshape.57), channel_id=1, replica_groups=mesh['col'=64,'row'=12] {'col'}, dimensions={0} | all-to-all | bytes 524288 | tf_op jit(solution)/shard_map/all_to_all | solution.py:262
  36.4 0.8 all_gather_reshape.3
  37.1 0.0 all-gather.2.cloned.1.call-update
  37.8 0.0 copy-done.6
  37.8 0.1 copy.13
  37.9 0.1 reshape.56.coords_ref
  38.0 0.1 pad_add_fusion.place_ref
  38.1 0.0 copy-done.2
  38.1 0.0 copy-start.3
  38.1 3.3 %shard_map.103 = (bf16[3,272,256]{2,1,0:T(8,128)(2,1)S(1)}, bf16[3,272,256]{2,1,0:T(8,128)(2,1)S(1)}, bf16[3,272,256]{2,1,0:T(8,128)(2,1)S(1)}, bf16[3,144,256]{2,1,0:T(8,128)(2,1)S(1)}, bf16[3,144,256]{2,1,0:T(8,128)(2,1)S(1)}) custom-call(s32[2]{0:T(128)S(1)} %pad_add_fusion.place_ref, s32[1]{0:T(128)S(6)} %copy.14.count_ref, s32[24]{0:T(128)S(1)} %reshape.56.coords_ref, ...), custom_call_target="tpu_custom_call" | custom-call | bytes 3145728 | tf_op jit(solution)/shard_map/pallas_call | solution.py:51
  41.4 1.9 collective-permute-start
  43.3 11.9 %collective-permute-start.1 = (bf16[3,272,256]{2,1,0:T(8,128)(2,1)S(1)}, bf16[3,272,256]{2,1,0:T(8,128)(2,1)S(1)}, u32[]{:S(2)}, u32[]{:S(2)}) collective-permute-start(bf16[3,272,256]{2,1,0:T(8,128)(2,1)S(1)} %get-tuple-element.18), channel_id=1, source_target_pairs={{0,1},{1,2},{2,3},{3,4},{4,5},{5,6},{6,7},{7,8},{8,9},{9,10},{10,1... | collective-permute-start | bytes 1253384 | tf_op jit(solution)/shard_map/ppermute | solution.py:256
  55.2 1.9 collective-permute-start.2
  57.1 5.5 %collective-permute-start.3 = (bf16[3,144,256]{2,1,0:T(8,128)(2,1)S(1)}, bf16[3,144,256]{2,1,0:T(8,128)(2,1)S(1)}, u32[]{:S(2)}, u32[]{:S(2)}) collective-permute-start(bf16[3,144,256]{2,1,0:T(8,128)(2,1)S(1)} %get-tuple-element.20), channel_id=1, source_target_pairs={{0,2},{1,3},{2,4},{3,5},{4,6},{5,7},{6,8},{7,9},{8,10},{9,11},{10,... | collective-permute-start | bytes 663560 | tf_op jit(solution)/shard_map/ppermute | solution.py:256
  62.6 14.5 %collective-permute-done.2.refs_3_ = bf16[3,144,256]{2,1,0:T(8,128)(2,1)S(1)} collective-permute-done((bf16[3,144,256]{2,1,0:T(8,128)(2,1)S(1)}, bf16[3,144,256]{2,1,0:T(8,128)(2,1)S(1)}, u32[]{:S(2)}, u32[]{:S(2)}) %collective-permute-start.2) | collective-permute-done | bytes 221216 | tf_op jit(solution)/shard_map/ppermute | solution.py:256
  77.0 7.7 %collective-permute-done.3.refs_4_ = bf16[3,144,256]{2,1,0:T(8,128)(2,1)S(1)} collective-permute-done((bf16[3,144,256]{2,1,0:T(8,128)(2,1)S(1)}, bf16[3,144,256]{2,1,0:T(8,128)(2,1)S(1)}, u32[]{:S(2)}, u32[]{:S(2)}) %collective-permute-start.3) | collective-permute-done | bytes 221216 | tf_op jit(solution)/shard_map/ppermute | solution.py:256
  84.7 0.0 collective-permute-done.refs_1_
  84.7 0.0 collective-permute-done.1.refs_2_
  84.7 21.7 %all-gather.2.cloned.1.call-done.refs_5_ = bf16[12,256,512]{2,1,0:T(8,128)(2,1)} async-done(((bf16[1,256,512]{2,1,0:T(8,128)(2,1)}), bf16[12,256,512]{2,1,0:T(8,128)(2,1)}) %all-gather.2.cloned.1.call-update) | async-done | bytes 3145744 | tf_op jit(solution)/shard_map/all_gather | solution.py:263
  106.4 1.9 copy-done.1
  108.3 3.5 %shard_map.104 = (f32[256,512]{1,0:T(8,128)S(1)}, bf16[256,512]{1,0:T(8,128)(2,1)S(1)}, bf16[256,512]{1,0:T(8,128)(2,1)S(1)}) custom-call(bf16[3,272,256]{2,1,0:T(8,128)(2,1)S(1)} %get-tuple-element.16.refs_0_, bf16[3,272,256]{2,1,0:T(8,128)(2,1)S(1)} %collective-permute-done.refs_1_, bf16[3,272,256]{2,1,0:T(8,128)(2,1)S(1)} %collective-permute-done.1.refs_2_, ...), custom_call_target="tpu_custom_call" | custom-call | flops 805306368 | bytes 6291456 | tf_op jit(solution)/shard_map/pallas_call | solution.py:95
  111.8 4.4 %collective-permute-start.4 = (bf16[256,512]{1,0:T(8,128)(2,1)S(1)}, bf16[256,512]{1,0:T(8,128)(2,1)S(1)}, u32[]{:S(2)}, u32[]{:S(2)}) collective-permute-start(bf16[256,512]{1,0:T(8,128)(2,1)S(1)} %get-tuple-element.22), channel_id=1, source_target_pairs={{0,4},{1,5},{2,6},{3,7},{4,8},{5,9},{6,10},{7,11},{8,0},{9,1},{10,... | collective-permute-start | bytes 786440 | tf_op jit(solution)/shard_map/ppermute | solution.py:256
  116.2 4.8 %collective-permute-start.5 = (bf16[256,512]{1,0:T(8,128)(2,1)S(1)}, bf16[256,512]{1,0:T(8,128)(2,1)S(1)}, u32[]{:S(2)}, u32[]{:S(2)}) collective-permute-start(bf16[256,512]{1,0:T(8,128)(2,1)S(1)} %get-tuple-element.23), channel_id=1, source_target_pairs={{0,8},{1,9},{2,10},{3,11},{4,0},{5,1},{6,2},{7,3},{8,4},{9,5},{10,... | collective-permute-start | bytes 786440 | tf_op jit(solution)/shard_map/ppermute | solution.py:256
  121.0 10.8 %collective-permute-done.4.refs_1_ = bf16[256,512]{1,0:T(8,128)(2,1)S(1)} collective-permute-done((bf16[256,512]{1,0:T(8,128)(2,1)S(1)}, bf16[256,512]{1,0:T(8,128)(2,1)S(1)}, u32[]{:S(2)}, u32[]{:S(2)}) %collective-permute-start.4) | collective-permute-done | bytes 262176 | tf_op jit(solution)/shard_map/ppermute | solution.py:256
  131.8 1.5 collective-permute-done.5.refs_2_
  133.3 0.0 copy-done.3
  133.3 0.0 copy-done.4
  133.3 0.0 copy-done.5
  133.3 1.4 shard_map.105
  134.7 5.7 %collective-permute-start.6 = (bf16[256,640]{1,0:T(8,128)(2,1)S(1)}, bf16[256,640]{1,0:T(8,128)(2,1)S(1)}, u32[]{:S(2)}, u32[]{:S(2)}) collective-permute-start(bf16[256,640]{1,0:T(8,128)(2,1)S(1)} %get-tuple-element.26), channel_id=1, source_target_pairs={{0,12},{12,0},{24,36},{36,24},{48,60},{60,48},{72,84},{84,72},{96,... | collective-permute-start | bytes 983048 | tf_op jit(solution)/shard_map/ppermute | solution.py:278
  140.5 1.2 collective-permute-done.6.right_ref
  141.7 0.1 shard_map.106
  141.8 23.9 %all_to_all.21.parts_ref = bf16[32,8,640]{2,1,0:T(8,128)(2,1)S(1)} all-to-all(bf16[32,8,640]{2,1,0:T(8,128)(2,1)S(1)} %bitcast.12), channel_id=1, replica_groups={{0,24,48,72,96,120,144,168,192,216,240,264,288,312,336,360,384,408,432,..., dimensions={0} | all-to-all | bytes 655360 | tf_op jit(solution)/shard_map/all_to_all | solution.py:280
  165.7 0.7 shard_map.107
  166.4 11.1 %all-to-all-start.2 = ((bf16[12,8,640]{2,1,0:T(8,128)(2,1)}), bf16[12,8,640]{2,1,0:T(8,128)(2,1)S(1)}, u32[]{:S(2)}, u32[]{:S(2)}) async-start(bf16[12,8,640]{2,1,0:T(8,128)(2,1)} %shard_map.107), calls=%async_computation.2 | async-start | bytes 245760 | tf_op jit(solution)/shard_map/all_to_all | solution.py:281
  177.5 10.4 %all-to-all-done.2.parts_ref = bf16[12,8,640]{2,1,0:T(8,128)(2,1)S(1)} async-done(((bf16[12,8,640]{2,1,0:T(8,128)(2,1)}), bf16[12,8,640]{2,1,0:T(8,128)(2,1)S(1)}, u32[]{:S(2)}, u32[]{:S(2)}) %all-to-all-start.2) | async-done | bytes 122912 | tf_op jit(solution)/shard_map/all_to_all | solution.py:281
  188.0 15.3 %all_to_all.22.mine_ref = bf16[32,8,640]{2,1,0:T(8,128)(2,1)S(1)} all-to-all(bf16[32,8,640]{2,1,0:T(8,128)(2,1)S(1)} %shard_map.108), channel_id=1, replica_groups={{0,24,48,72,96,120,144,168,192,216,240,264,288,312,336,360,384,408,432,..., dimensions={0} | all-to-all | bytes 655360 | tf_op jit(solution)/shard_map/all_to_all | solution.py:283
  203.3 6.5 %collective-permute-start.7 = (bf16[32,8,640]{2,1,0:T(8,128)(2,1)S(1)}, bf16[32,8,640]{2,1,0:T(8,128)(2,1)S(1)}, u32[]{:S(2)}, u32[]{:S(2)}) collective-permute-start(bf16[32,8,640]{2,1,0:T(8,128)(2,1)S(1)} %all_to_all.22.mine_ref), channel_id=1, source_target_pairs={{0,12},{12,0},{24,36},{36,24},{48,60},{60,48},{72,84},{84,72},{96,... | collective-permute-start | bytes 983048 | tf_op jit(solution)/shard_map/ppermute | solution.py:284
  209.8 1.2 collective-permute-done.7.other_ref
  211.0 1.0 shard_map.109
  (5 shorter events, 0.1 us)
Async XLA Ops:
  7.2 1.0 copy-start
  7.2 30.6 %copy-start.6 = (s32[1,12,2]{1,2,0:T(2,128)S(1)}, s32[1,12,2]{1,2,0:T(2,128)}, u32[]{:S(2)}) copy-start(s32[1,12,2]{1,2,0:T(2,128)} %param.11) | copy-start | bytes 292
  7.2 30.9 %copy-start.2 = (bf16[1,12,256,256]{3,2,1,0:T(8,128)(2,1)S(1)}, bf16[1,12,256,256]{3,2,1,0:T(8,128)(2,1)}, u32[]{:S(2)}) copy-start(bf16[1,12,256,256]{3,2,1,0:T(8,128)(2,1)} %param.10) | copy-start | bytes 4718596
  7.2 99.2 %all-gather.2.cloned.1.call-start = ((), (), s32[]{:S(2)}) async-start(), calls=%async_computation.4 | async-start | bytes 3407872 | tf_op jit(solution)/shard_map/all_gather | solution.py:263
  38.1 95.2 %copy-start.3 = (bf16[512,512]{1,0:T(8,128)(2,1)S(1)}, bf16[512,512]{1,0:T(8,128)(2,1)}, u32[]{:S(2)}) copy-start(bf16[512,512]{1,0:T(8,128)(2,1)} %refs_3_.1) | copy-start | bytes 1572868
  38.1 95.2 %copy-start.4 = (bf16[256,512]{1,0:T(8,128)(2,1)S(1)}, bf16[256,512]{1,0:T(8,128)(2,1)}, u32[]{:S(2)}) copy-start(bf16[256,512]{1,0:T(8,128)(2,1)} %refs_5_.1) | copy-start | bytes 786436
  38.1 95.2 %copy-start.5 = (f32[512]{0:T(512)S(1)}, f32[512]{0:T(512)}, u32[]{:S(2)}) copy-start(f32[512]{0:T(512)} %param.14) | copy-start | bytes 6148
  41.4 43.3 %collective-permute-start = (bf16[3,272,256]{2,1,0:T(8,128)(2,1)S(1)}, bf16[3,272,256]{2,1,0:T(8,128)(2,1)S(1)}, u32[]{:S(2)}, u32[]{:S(2)}) collective-permute-start(bf16[3,272,256]{2,1,0:T(8,128)(2,1)S(1)} %get-tuple-element.17), channel_id=1, source_target_pairs={{0,11},{1,0},{2,1},{3,2},{4,3},{5,4},{6,5},{7,6},{8,7},{9,8},{10,9... | collective-permute-start | bytes 1253384 | tf_op jit(solution)/shard_map/ppermute | solution.py:256
  43.3 41.4 %collective-permute-start.1 = (bf16[3,272,256]{2,1,0:T(8,128)(2,1)S(1)}, bf16[3,272,256]{2,1,0:T(8,128)(2,1)S(1)}, u32[]{:S(2)}, u32[]{:S(2)}) collective-permute-start(bf16[3,272,256]{2,1,0:T(8,128)(2,1)S(1)} %get-tuple-element.18), channel_id=1, source_target_pairs={{0,1},{1,2},{2,3},{3,4},{4,5},{5,6},{6,7},{7,8},{8,9},{9,10},{10,1... | collective-permute-start | bytes 1253384 | tf_op jit(solution)/shard_map/ppermute | solution.py:256
  55.2 21.9 %collective-permute-start.2 = (bf16[3,144,256]{2,1,0:T(8,128)(2,1)S(1)}, bf16[3,144,256]{2,1,0:T(8,128)(2,1)S(1)}, u32[]{:S(2)}, u32[]{:S(2)}) collective-permute-start(bf16[3,144,256]{2,1,0:T(8,128)(2,1)S(1)} %get-tuple-element.19), channel_id=1, source_target_pairs={{0,10},{1,11},{2,0},{3,1},{4,2},{5,3},{6,4},{7,5},{8,6},{9,7},{10,... | collective-permute-start | bytes 663560 | tf_op jit(solution)/shard_map/ppermute | solution.py:256
  57.1 27.6 %collective-permute-start.3 = (bf16[3,144,256]{2,1,0:T(8,128)(2,1)S(1)}, bf16[3,144,256]{2,1,0:T(8,128)(2,1)S(1)}, u32[]{:S(2)}, u32[]{:S(2)}) collective-permute-start(bf16[3,144,256]{2,1,0:T(8,128)(2,1)S(1)} %get-tuple-element.20), channel_id=1, source_target_pairs={{0,2},{1,3},{2,4},{3,5},{4,6},{5,7},{6,8},{7,9},{8,10},{9,11},{10,... | collective-permute-start | bytes 663560 | tf_op jit(solution)/shard_map/ppermute | solution.py:256
  106.4 1.9 copy-start.1
  111.8 20.0 %collective-permute-start.4 = (bf16[256,512]{1,0:T(8,128)(2,1)S(1)}, bf16[256,512]{1,0:T(8,128)(2,1)S(1)}, u32[]{:S(2)}, u32[]{:S(2)}) collective-permute-start(bf16[256,512]{1,0:T(8,128)(2,1)S(1)} %get-tuple-element.22), channel_id=1, source_target_pairs={{0,4},{1,5},{2,6},{3,7},{4,8},{5,9},{6,10},{7,11},{8,0},{9,1},{10,... | collective-permute-start | bytes 786440 | tf_op jit(solution)/shard_map/ppermute | solution.py:256
  116.2 17.1 %collective-permute-start.5 = (bf16[256,512]{1,0:T(8,128)(2,1)S(1)}, bf16[256,512]{1,0:T(8,128)(2,1)S(1)}, u32[]{:S(2)}, u32[]{:S(2)}) collective-permute-start(bf16[256,512]{1,0:T(8,128)(2,1)S(1)} %get-tuple-element.23), channel_id=1, source_target_pairs={{0,8},{1,9},{2,10},{3,11},{4,0},{5,1},{6,2},{7,3},{8,4},{9,5},{10,... | collective-permute-start | bytes 786440 | tf_op jit(solution)/shard_map/ppermute | solution.py:256
  134.7 7.0 %collective-permute-start.6 = (bf16[256,640]{1,0:T(8,128)(2,1)S(1)}, bf16[256,640]{1,0:T(8,128)(2,1)S(1)}, u32[]{:S(2)}, u32[]{:S(2)}) collective-permute-start(bf16[256,640]{1,0:T(8,128)(2,1)S(1)} %get-tuple-element.26), channel_id=1, source_target_pairs={{0,12},{12,0},{24,36},{36,24},{48,60},{60,48},{72,84},{84,72},{96,... | collective-permute-start | bytes 983048 | tf_op jit(solution)/shard_map/ppermute | solution.py:278
  166.4 21.5 %all-to-all-start.2 = ((bf16[12,8,640]{2,1,0:T(8,128)(2,1)}), bf16[12,8,640]{2,1,0:T(8,128)(2,1)S(1)}, u32[]{:S(2)}, u32[]{:S(2)}) async-start(bf16[12,8,640]{2,1,0:T(8,128)(2,1)} %shard_map.107), calls=%async_computation.2 | async-start | bytes 245760 | tf_op jit(solution)/shard_map/all_to_all | solution.py:281
  203.3 7.7 %collective-permute-start.7 = (bf16[32,8,640]{2,1,0:T(8,128)(2,1)S(1)}, bf16[32,8,640]{2,1,0:T(8,128)(2,1)S(1)}, u32[]{:S(2)}, u32[]{:S(2)}) collective-permute-start(bf16[32,8,640]{2,1,0:T(8,128)(2,1)S(1)} %all_to_all.22.mine_ref), channel_id=1, source_target_pairs={{0,12},{12,0},{24,36},{36,24},{48,60},{60,48},{72,84},{84,72},{96,... | collective-permute-start | bytes 983048 | tf_op jit(solution)/shard_map/ppermute | solution.py:284
Sparse Core Ops, SparseCore 0:
  37.3 69.0 all-gather.1

commit v3 on v2

--- a/solution.py
+++ b/solution.py
@@ -12,8 +12,7 @@
 LANES = 128
 META_ROWS = 16
 STRIDE = 4
-STRIDE = 4
-ROUTES = ((0, 0, 2), (1, 0, 2), (-1, 0, 2), (2, 0, 1), (-2, 1, 2))
+TIE = 1
 VMEM_LIMIT = 16 * 1024 * 1024
 IN_VMEM = pl.BlockSpec(memory_space=pltpu.VMEM)
 IN_SMEM = pl.BlockSpec(memory_space=pltpu.SMEM)
@@ -21,45 +20,52 @@
 PARAMS = pltpu.CompilerParams(vmem_limit_bytes=VMEM_LIMIT)
 
 
+def ring_place(place_ref, n):
+    here, turn = place_ref[0], place_ref[1]
+    near = jnp.where(lax.rem(here, 2) == 0, 1, -1)
+    far = jnp.where(lax.rem(lax.div(lax.rem(here * turn + n, n), 2), 2) == 0, 1, -1)
+    return here, turn, near, far
+
+
+def routes(near, far):
+    return (0, near, -near, 2 * far)
+
+
 def bundle_tiles(place, count, coords, tile_set):
     n, rows, columns = tile_set.shape
-    size, half = n // STRIDE, rows // 2
-    heights = [(last - begin) * half for _, begin, last in ROUTES]
-    pieces = len(heights) * size
+    size = n // STRIDE
 
     def kernel(place_ref, count_ref, coords_ref, tiles_ref, *refs):
-        out_refs, (meta, tile_sems, meta_sems) = refs[: len(heights)], refs[len(heights) :]
-        here, turn, first = place_ref[0], place_ref[1], coords_ref[0]
+        out_refs, (meta, tile_sems, meta_sems) = refs[:STRIDE], refs[STRIDE:]
+        here, turn, near, far = ring_place(place_ref, n)
+        first = coords_ref[0]
         copies = []
-        for g, (behind, begin, _) in enumerate(ROUTES):
+        for g, ahead in enumerate(routes(near, far)):
             for p in range(size):
                 i = g * size + p
-                output = here + turn * (p * STRIDE - behind)
+                output = here + turn * (p * STRIDE + ahead)
                 slot = lax.rem(output - first + 3 * n, n)
-                source = tiles_ref.at[slot, pl.ds(begin * half, heights[g])]
-                target = out_refs[g].at[p, pl.ds(0, heights[g])]
-                copies.append(pltpu.make_async_copy(source, target, tile_sems.at[i]))
+                target = out_refs[g].at[p, pl.ds(0, rows)]
+                copies.append(pltpu.make_async_copy(tiles_ref.at[slot], target, tile_sems.at[i]))
                 copies[-1].start()
                 block = jnp.where(slot < count_ref[0], coords_ref[2 * slot + 1], -1)
                 meta[i] = jnp.full(meta.shape[1:], block.astype(F32), F32).astype(BF16)
-                note = out_refs[g].at[p, pl.ds(heights[g], META_ROWS)]
+                note = out_refs[g].at[p, pl.ds(rows, META_ROWS)]
                 copies.append(pltpu.make_async_copy(meta.at[i], note, meta_sems.at[i]))
                 copies[-1].start()
         for copy in copies:
             copy.wait()
 
-    return pl.pallas_call(
-        kernel,
-        out_shape=[
-            jax.ShapeDtypeStruct((size, height + META_ROWS, columns), tile_set.dtype)
-            for height in heights
-        ],
+    bundle = jax.ShapeDtypeStruct((size, rows + META_ROWS, columns), tile_set.dtype)
+    return pl.pallas_call(
+        kernel,
+        out_shape=[bundle] * STRIDE,
         in_specs=[IN_SMEM] * 3 + [IN_PLACE],
-        out_specs=[IN_PLACE] * len(heights),
+        out_specs=[IN_PLACE] * STRIDE,
         scratch_shapes=[
-            pltpu.VMEM((pieces, META_ROWS, columns), tile_set.dtype),
-            pltpu.SemaphoreType.DMA((pieces,)),
-            pltpu.SemaphoreType.DMA((pieces,)),
+            pltpu.VMEM((n, META_ROWS, columns), tile_set.dtype),
+            pltpu.SemaphoreType.DMA((n,)),
+            pltpu.SemaphoreType.DMA((n,)),
         ],
         compiler_params=PARAMS,
         cost_estimate=pl.CostEstimate(
@@ -68,26 +74,34 @@
     )(place, count, coords, tile_set)
 
 
-def partial_sums(bundles, blocks):
+def partial_sums(place, bundles, blocks):
     groups, size = len(bundles), bundles[0].shape[0]
-    n, rows, width = blocks.shape
-    half = rows // 2
-
-    def kernel(*refs):
-        bundle_refs, blocks_ref = refs[:groups], refs[groups]
-        out_refs, sums = refs[groups + 1 : -1], refs[-1]
+    n = len(blocks)
+    rows, width = blocks[0].shape
+
+    def kernel(place_ref, *refs):
+        bundle_refs = refs[:groups]
+        block_refs = refs[groups : groups + n]
+        out_refs = refs[groups + n : -2]
+        sums, which = refs[-2:]
+        here, turn, near, _ = ring_place(place_ref, n)
+        for g, bundle_ref in enumerate(bundle_refs):
+            for p in range(size):
+                note = bundle_ref[p, rows : rows + META_ROWS, :LANES].astype(F32)
+                block = jnp.max(note).astype(jnp.int32)
+                away = lax.rem(near * turn * (block - here) + n, n)
+                which[g * size + p] = jnp.where(block < 0, -1, away)
         sums[...] = jnp.zeros_like(sums)
-        for p in range(size):
-            for bundle_ref, (_, begin, last) in zip(bundle_refs, ROUTES):
-                height = (last - begin) * half
-                note = bundle_ref[p, height : height + META_ROWS, :LANES].astype(F32)
-                block = jnp.max(note).astype(jnp.int32)
-
-                @pl.when(block >= 0)
-                def _():
-                    sums[p, begin * half : last * half, :] += jnp.dot(
-                        bundle_ref[p, :height, :], blocks_ref[block], preferred_element_type=F32
-                    )
+        for d, block_ref in enumerate(block_refs):
+            for g, bundle_ref in enumerate(bundle_refs):
+
+                @pl.loop(0, size)
+                def _(p):
+                    @pl.when(which[g * size + p] == d)
+                    def _():
+                        sums[p] += jnp.dot(
+                            bundle_ref[p, :rows, :], block_ref[...], preferred_element_type=F32
+                        )
 
         for p, out_ref in enumerate(out_refs):
             out_ref[...] = sums[p].astype(out_ref.dtype)
@@ -97,16 +111,19 @@
         out_shape=[
             jax.ShapeDtypeStruct((rows, width), F32 if p == 0 else BF16) for p in range(size)
         ],
-        in_specs=[IN_VMEM] * (groups + 1),
+        in_specs=[IN_SMEM] + [IN_VMEM] * (groups + n),
         out_specs=[IN_VMEM] * size,
-        scratch_shapes=[pltpu.VMEM((size, rows, width), F32)],
+        scratch_shapes=[
+            pltpu.VMEM((size, rows, width), F32),
+            pltpu.SMEM((groups * size,), jnp.int32),
+        ],
         compiler_params=PARAMS,
         cost_estimate=pl.CostEstimate(
             flops=2 * n * rows * rows * width,
             bytes_accessed=6 * 1024 * 1024,
             transcendentals=0,
         ),
-    )(*bundles, blocks)
+    )(place, *bundles, *blocks)
 
 
 def layer(core, sums, weight, bias, cotangent):
@@ -255,19 +272,28 @@
                 pairs.append((col * row_count + row, col * row_count + target))
         return lax.ppermute(x, ("col", "row"), pairs)
 
+    def swap(x, side, reach=1):
+        return permute(x, lambda row: reach if row // reach % 2 == side else -reach)
+
     col, row = (lax.axis_index(axis).astype(jnp.int32) for axis in ("col", "row"))
     place = jnp.stack([row, 1 - 2 * lax.rem(col, 2)])
 
+    bundles = bundle_tiles(place, counts, coords.reshape(-1), tiles[0])
+    bundles = [bundles[0], swap(bundles[1], 0), swap(bundles[2], 1), swap(bundles[3], 0, 2)]
     sent = features[pick[0]].reshape(col_count, slot_rows, width)
     blocked = exchange(sent, "col").reshape(block_rows, width)
-    blocks = lax.all_gather(blocked, "row", axis=0)
-
-    bundles = bundle_tiles(place, counts, coords.reshape(-1), tiles[0])
-    bundles = [
-        permute(x, lambda _, behind=route[0]: -behind) if route[0] else x
-        for x, route in zip(bundles, ROUTES)
-    ]
-    sums = partial_sums(bundles, blocks)
+
+    blocks = [blocked] + [None] * (row_count - 1)
+    ahead = behind = blocked
+    for step in range(1, row_count // 2 + 1):
+        ahead, behind = swap(behind, 0), swap(ahead, 1) if 2 * step < row_count else None
+        if step == TIE:
+            ahead, behind, *bundles = lax.optimization_barrier((ahead, behind, *bundles))
+        blocks[step] = ahead
+        if behind is not None:
+            blocks[row_count - step] = behind
+
+    sums = partial_sums(place, bundles, blocks)
     sums = [sums[0]] + [permute(sums[p], lambda _, p=p: p * STRIDE) for p in range(1, len(sums))]
     core = lax.rem(col, 2).reshape(1)
     hidden, keep, give = layer(core, sums, weight, bias.reshape(1, width), cotangent)

time: 220 us -> 211 us (0.959)
  starting transfers between devices: 53.7 us -> 93.6 us
  blocking collectives: 66.2 us -> 42.4 us
  between operations: 14.8 us -> 1.57 us
  waiting for transfers between devices: 69 us -> 57.2 us
    ppermute x6 -> x16, starting transfers between devices: 30.4 us -> 60.3 us  [permute(): return lax.ppermute(x, ('col', 'row'), pairs)]
    all_to_all x1 -> x0, blocking collectives: 27 us -> none  [on_device(): blocked = exchange(sent, 'col').reshape(block_rows, width)]
    all_gather x1 -> x0, waiting for transfers between devices: 21.7 us -> none  [on_device(): blocks = lax.all_gather(blocked, 'row', axis=0)]
    all_to_all x0 -> x1, starting transfers between devices: none -> 15.4 us  [on_device(): blocked = exchange(sent, 'col').reshape(block_rows, width)]
    ppermute x6 -> x16, waiting for transfers between devices: 34.4 us -> 44.3 us  [permute(): return lax.ppermute(x, ('col', 'row'), pairs)]
    all_to_all x1, starting transfers between devices: 11.1 us -> 5.23 us  [on_device(): parts = exchange(sum_over_chips(parts, row_count), 'row')]
    all_to_all x1, blocking collectives: 23.9 us -> 27.1 us  [on_device(): parts = exchange(parts, 'col', axis_index_groups=cores)]
  transfers between devices with their start and end apart: 10 -> 20, of which waited for: 8 -> 14; matrix products, arithmetic and copies ran while one was open for 0% -> 1% of each run, Pallas kernels for 1% -> 2%
where the time goes in v3:
time: 211 us; the launch traced here: 210 us
  starting transfers between devices  93.6 us (44%)
  waiting for transfers between devices  57.2 us (27%)
  blocking collectives  42.4 us (20%)
  Pallas kernels  11 us (5%)
  local copies, waits for them, and re-layouts  3.37 us (2%)
    ppermute x16, starting transfers between devices, permute(): return lax.ppermute(x, ('col', 'row'), pairs)  60.3 us
    ppermute x16, waiting for transfers between devices, permute(): return lax.ppermute(x, ('col', 'row'), pairs)  44.3 us
    all_to_all x1, blocking collectives, on_device(): parts = exchange(parts, 'col', axis_index_groups=cores)  27.1 us
    all_to_all x1, starting transfers between devices, on_device(): blocked = exchange(sent, 'col').reshape(block_rows, width)  15.4 us
    all_to_all x1, blocking collectives, on_device(): mine = exchange(parts, 'col', axis_index_groups=cores)  15.3 us
    all_to_all x1, waiting for transfers between devices, on_device(): parts = exchange(sum_over_chips(parts, row_count), 'row')  10.4 us
    ppermute x1, starting transfers between devices, on_device(): other = lax.ppermute(mine, 'col', other_core)  6.49 us
    ppermute x1, starting transfers between devices, on_device(): parts = sum_two(keep, lax.ppermute(give, 'col', other_core))  6.22 us
  transfers between devices with their start and end apart: 20, of which 14 were waited for; matrix products, arithmetic and copies ran while one was open for 1% of the time, Pallas kernels for 2%

profile of v3, /device:TPU:1, one launch (start us, length us, event | category | flops | bytes accessed | tf_op | source)
XLA Modules:
  0.0 209.9 jit_solution(5174144258665701928)
XLA Ops:
  0.6 0.7 compare_select_fusion
  1.4 0.2 copy-done
  1.6 1.2 gather_fusion
  2.8 0.8 reshape.59
  3.5 15.4 %all-to-all-start = ((bf16[64,4,512]{2,1,0:T(4,128)(2,1)}), bf16[64,4,512]{2,1,0:T(4,128)(2,1)}, u32[]{:S(2)}, u32[]{:S(2)}) async-start(bf16[64,4,512]{2,1,0:T(4,128)(2,1)} %reshape.59), calls=%async_computation | async-start | bytes 524288 | tf_op jit(solution)/shard_map/all_to_all | solution.py:284
  19.6 0.1 copy.12
  19.7 0.1 reshape.61.coords_ref
  19.8 3.2 %shard_map.103 = (bf16[3,272,256]{2,1,0:T(8,128)(2,1)S(1)}, bf16[3,272,256]{2,1,0:T(8,128)(2,1)S(1)}, bf16[3,272,256]{2,1,0:T(8,128)(2,1)S(1)}, bf16[3,272,256]{2,1,0:T(8,128)(2,1)S(1)}) custom-call(s32[2]{0:T(128)S(1)} %pad_add_fusion.place_ref, s32[1]{0:T(128)S(6)} %copy.13.count_ref, s32[24]{0:T(128)S(1)} %reshape.61.coords_ref, ...), custom_call_target="tpu_custom_call" | custom-call | bytes 3145728 | tf_op jit(solution)/shard_map/pallas_call | solution.py:60
  23.0 10.8 %collective-permute-start.2 = (bf16[3,272,256]{2,1,0:T(8,128)(2,1)S(1)}, bf16[3,272,256]{2,1,0:T(8,128)(2,1)S(1)}, u32[]{:S(2)}, u32[]{:S(2)}) collective-permute-start(bf16[3,272,256]{2,1,0:T(8,128)(2,1)S(1)} %get-tuple-element.22), channel_id=1, source_target_pairs={{0,1},{1,0},{2,3},{3,2},{4,5},{5,4},{6,7},{7,6},{8,9},{9,8},{10,11... | collective-permute-start | bytes 1253384 | tf_op jit(solution)/shard_map/ppermute | solution.py:273
  33.8 1.9 collective-permute-start.3
  35.7 3.1 %collective-permute-start.4 = (bf16[3,272,256]{2,1,0:T(8,128)(2,1)S(1)}, bf16[3,272,256]{2,1,0:T(8,128)(2,1)S(1)}, u32[]{:S(2)}, u32[]{:S(2)}) collective-permute-start(bf16[3,272,256]{2,1,0:T(8,128)(2,1)S(1)} %get-tuple-element.24), channel_id=1, source_target_pairs={{0,2},{1,3},{2,0},{3,1},{4,6},{5,7},{6,4},{7,5},{8,10},{9,11},{10,... | collective-permute-start | bytes 1253384 | tf_op jit(solution)/shard_map/ppermute | solution.py:273
  38.8 1.0 reshape.60.refs_4_
  39.8 2.2 %collective-permute-start.1 = (bf16[256,512]{1,0:T(8,128)(2,1)S(1)}, bf16[256,512]{1,0:T(8,128)(2,1)S(1)}, u32[]{:S(2)}, u32[]{:S(2)}) collective-permute-start(bf16[256,512]{1,0:T(8,128)(2,1)S(1)} %reshape.60.refs_4_), channel_id=1, source_target_pairs={{0,11},{1,2},{2,1},{3,4},{4,3},{5,6},{6,5},{7,8},{8,7},{9,10},{10,... | collective-permute-start | bytes 786440 | tf_op jit(solution)/shard_map/ppermute | solution.py:273
  42.0 4.3 %collective-permute-start = (bf16[256,512]{1,0:T(8,128)(2,1)S(1)}, bf16[256,512]{1,0:T(8,128)(2,1)S(1)}, u32[]{:S(2)}, u32[]{:S(2)}) collective-permute-start(bf16[256,512]{1,0:T(8,128)(2,1)S(1)} %reshape.60.refs_4_), channel_id=1, source_target_pairs={{0,1},{1,0},{2,3},{3,2},{4,5},{5,4},{6,7},{7,6},{8,9},{9,8},{10,11... | collective-permute-start | bytes 786440 | tf_op jit(solution)/shard_map/ppermute | solution.py:273
  46.3 15.7 %collective-permute-done.4.refs_3_ = bf16[3,272,256]{2,1,0:T(8,128)(2,1)S(1)} collective-permute-done((bf16[3,272,256]{2,1,0:T(8,128)(2,1)S(1)}, bf16[3,272,256]{2,1,0:T(8,128)(2,1)S(1)}, u32[]{:S(2)}, u32[]{:S(2)}) %collective-permute-start.4) | collective-permute-done | bytes 417824 | tf_op jit(solution)/shard_map/ppermute | solution.py:273
  62.1 5.1 %collective-permute-start.5 = (bf16[256,512]{1,0:T(8,128)(2,1)S(1)}, bf16[256,512]{1,0:T(8,128)(2,1)S(1)}, u32[]{:S(2)}, u32[]{:S(2)}) collective-permute-start(bf16[256,512]{1,0:T(8,128)(2,1)S(1)} %collective-permute-done.1.refs_15_), channel_id=1, source_target_pairs={{0,1},{1,0},{2,3},{3,2},{4,5},{5,4},{6,7},{7,6},{8,9},{9,8},{10,11... | collective-permute-start | bytes 786440 | tf_op jit(solution)/shard_map/ppermute | solution.py:273
  67.2 1.9 collective-permute-start.6
  69.1 2.5 %collective-permute-done.5.refs_6_ = bf16[256,512]{1,0:T(8,128)(2,1)S(1)} collective-permute-done((bf16[256,512]{1,0:T(8,128)(2,1)S(1)}, bf16[256,512]{1,0:T(8,128)(2,1)S(1)}, u32[]{:S(2)}, u32[]{:S(2)}) %collective-permute-start.5) | collective-permute-done | bytes 262176 | tf_op jit(solution)/shard_map/ppermute | solution.py:273
  71.6 1.9 collective-permute-start.8
  73.5 0.8 collective-permute-done.6.refs_14_
  74.3 3.5 %collective-permute-start.7 = (bf16[256,512]{1,0:T(8,128)(2,1)S(1)}, bf16[256,512]{1,0:T(8,128)(2,1)S(1)}, u32[]{:S(2)}, u32[]{:S(2)}) collective-permute-start(bf16[256,512]{1,0:T(8,128)(2,1)S(1)} %collective-permute-done.6.refs_14_), channel_id=1, source_target_pairs={{0,1},{1,0},{2,3},{3,2},{4,5},{5,4},{6,7},{7,6},{8,9},{9,8},{10,11... | collective-permute-start | bytes 786440 | tf_op jit(solution)/shard_map/ppermute | solution.py:273
  77.9 0.9 collective-permute-done.8.refs_13_
  78.7 4.5 %collective-permute-start.9 = (bf16[256,512]{1,0:T(8,128)(2,1)S(1)}, bf16[256,512]{1,0:T(8,128)(2,1)S(1)}, u32[]{:S(2)}, u32[]{:S(2)}) collective-permute-start(bf16[256,512]{1,0:T(8,128)(2,1)S(1)} %collective-permute-done.8.refs_13_), channel_id=1, source_target_pairs={{0,1},{1,0},{2,3},{3,2},{4,5},{5,4},{6,7},{7,6},{8,9},{9,8},{10,11... | collective-permute-start | bytes 786440 | tf_op jit(solution)/shard_map/ppermute | solution.py:273
  83.2 1.9 collective-permute-start.10
  85.2 1.9 collective-permute-done.9.refs_8_
  87.1 1.9 collective-permute-start.12
  89.0 1.7 collective-permute-done.10.refs_12_
  90.6 3.6 %collective-permute-start.11 = (bf16[256,512]{1,0:T(8,128)(2,1)S(1)}, bf16[256,512]{1,0:T(8,128)(2,1)S(1)}, u32[]{:S(2)}, u32[]{:S(2)}) collective-permute-start(bf16[256,512]{1,0:T(8,128)(2,1)S(1)} %collective-permute-done.10.refs_12_), channel_id=1, source_target_pairs={{0,1},{1,0},{2,3},{3,2},{4,5},{5,4},{6,7},{7,6},{8,9},{9,8},{10,11... | collective-permute-start | bytes 786440 | tf_op jit(solution)/shard_map/ppermute | solution.py:273
  94.3 0.2 collective-permute-done.12.refs_11_
  94.5 4.5 %collective-permute-start.13 = (bf16[256,512]{1,0:T(8,128)(2,1)S(1)}, bf16[256,512]{1,0:T(8,128)(2,1)S(1)}, u32[]{:S(2)}, u32[]{:S(2)}) collective-permute-start(bf16[256,512]{1,0:T(8,128)(2,1)S(1)} %collective-permute-done.12.refs_11_), channel_id=1, source_target_pairs={{0,1},{1,0},{2,3},{3,2},{4,5},{5,4},{6,7},{7,6},{8,9},{9,8},{10,11... | collective-permute-start | bytes 786440 | tf_op jit(solution)/shard_map/ppermute | solution.py:273
  98.9 0.3 collective-permute-done.11.refs_9_
  99.3 3.5 %collective-permute-done.13.refs_10_ = bf16[256,512]{1,0:T(8,128)(2,1)S(1)} collective-permute-done((bf16[256,512]{1,0:T(8,128)(2,1)S(1)}, bf16[256,512]{1,0:T(8,128)(2,1)S(1)}, u32[]{:S(2)}, u32[]{:S(2)}) %collective-permute-start.13) | collective-permute-done | bytes 262176 | tf_op jit(solution)/shard_map/ppermute | solution.py:273
  102.8 4.5 %shard_map.104 = (f32[256,512]{1,0:T(8,128)S(1)}, bf16[256,512]{1,0:T(8,128)(2,1)S(1)}, bf16[256,512]{1,0:T(8,128)(2,1)S(1)}) custom-call(s32[2]{0:T(128)S(1)} %pad_add_fusion.place_ref, bf16[3,272,256]{2,1,0:T(8,128)(2,1)S(1)} %get-tuple-element.25.refs_0_, bf16[3,272,256]{2,1,0:T(8,128)(2,1)S(1)} %collective-permute-done.2.refs_1_, ...), custom_call_target="tpu_custom_call" | custom-call | flops 805306368 | bytes 6291456 | tf_op jit(solution)/shard_map/pallas_call | solution.py:109
  107.3 5.1 %collective-permute-start.14 = (bf16[256,512]{1,0:T(8,128)(2,1)S(1)}, bf16[256,512]{1,0:T(8,128)(2,1)S(1)}, u32[]{:S(2)}, u32[]{:S(2)}) collective-permute-start(bf16[256,512]{1,0:T(8,128)(2,1)S(1)} %get-tuple-element.32), channel_id=1, source_target_pairs={{0,4},{1,5},{2,6},{3,7},{4,8},{5,9},{6,10},{7,11},{8,0},{9,1},{10,... | collective-permute-start | bytes 786440 | tf_op jit(solution)/shard_map/ppermute | solution.py:273
  112.4 4.0 %collective-permute-start.15 = (bf16[256,512]{1,0:T(8,128)(2,1)S(1)}, bf16[256,512]{1,0:T(8,128)(2,1)S(1)}, u32[]{:S(2)}, u32[]{:S(2)}) collective-permute-start(bf16[256,512]{1,0:T(8,128)(2,1)S(1)} %get-tuple-element.33), channel_id=1, source_target_pairs={{0,8},{1,9},{2,10},{3,11},{4,0},{5,1},{6,2},{7,3},{8,4},{9,5},{10,... | collective-permute-start | bytes 786440 | tf_op jit(solution)/shard_map/ppermute | solution.py:273
  116.5 12.1 %collective-permute-done.14.refs_1_ = bf16[256,512]{1,0:T(8,128)(2,1)S(1)} collective-permute-done((bf16[256,512]{1,0:T(8,128)(2,1)S(1)}, bf16[256,512]{1,0:T(8,128)(2,1)S(1)}, u32[]{:S(2)}, u32[]{:S(2)}) %collective-permute-start.14) | collective-permute-done | bytes 262176 | tf_op jit(solution)/shard_map/ppermute | solution.py:273
  128.6 4.7 %collective-permute-done.15.refs_2_ = bf16[256,512]{1,0:T(8,128)(2,1)S(1)} collective-permute-done((bf16[256,512]{1,0:T(8,128)(2,1)S(1)}, bf16[256,512]{1,0:T(8,128)(2,1)S(1)}, u32[]{:S(2)}, u32[]{:S(2)}) %collective-permute-start.15) | collective-permute-done | bytes 262176 | tf_op jit(solution)/shard_map/ppermute | solution.py:273
  133.3 1.4 shard_map.105
  134.8 6.2 %collective-permute-start.16 = (bf16[256,640]{1,0:T(8,128)(2,1)S(1)}, bf16[256,640]{1,0:T(8,128)(2,1)S(1)}, u32[]{:S(2)}, u32[]{:S(2)}) collective-permute-start(bf16[256,640]{1,0:T(8,128)(2,1)S(1)} %get-tuple-element.36), channel_id=1, source_target_pairs={{0,12},{12,0},{24,36},{36,24},{48,60},{60,48},{72,84},{84,72},{96,... | collective-permute-start | bytes 983048 | tf_op jit(solution)/shard_map/ppermute | solution.py:304
  141.0 1.2 collective-permute-done.16.right_ref
  142.3 27.1 %all_to_all.20.parts_ref = bf16[32,8,640]{2,1,0:T(8,128)(2,1)S(1)} all-to-all(bf16[32,8,640]{2,1,0:T(8,128)(2,1)S(1)} %bitcast.12), channel_id=1, replica_groups={{0,24,48,72,96,120,144,168,192,216,240,264,288,312,336,360,384,408,432,..., dimensions={0} | all-to-all | bytes 655360 | tf_op jit(solution)/shard_map/all_to_all | solution.py:306
  169.4 0.7 shard_map.107
  170.1 5.2 %all-to-all-start.2 = ((bf16[12,8,640]{2,1,0:T(8,128)(2,1)}), bf16[12,8,640]{2,1,0:T(8,128)(2,1)S(1)}, u32[]{:S(2)}, u32[]{:S(2)}) async-start(bf16[12,8,640]{2,1,0:T(8,128)(2,1)} %shard_map.107), calls=%async_computation.2 | async-start | bytes 245760 | tf_op jit(solution)/shard_map/all_to_all | solution.py:307
  175.4 10.4 %all-to-all-done.2.parts_ref = bf16[12,8,640]{2,1,0:T(8,128)(2,1)S(1)} async-done(((bf16[12,8,640]{2,1,0:T(8,128)(2,1)}), bf16[12,8,640]{2,1,0:T(8,128)(2,1)S(1)}, u32[]{:S(2)}, u32[]{:S(2)}) %all-to-all-start.2) | async-done | bytes 122912 | tf_op jit(solution)/shard_map/all_to_all | solution.py:307
  185.8 15.3 %all_to_all.21.mine_ref = bf16[32,8,640]{2,1,0:T(8,128)(2,1)S(1)} all-to-all(bf16[32,8,640]{2,1,0:T(8,128)(2,1)S(1)} %shard_map.108), channel_id=1, replica_groups={{0,24,48,72,96,120,144,168,192,216,240,264,288,312,336,360,384,408,432,..., dimensions={0} | all-to-all | bytes 655360 | tf_op jit(solution)/shard_map/all_to_all | solution.py:309
  201.1 6.5 %collective-permute-start.17 = (bf16[32,8,640]{2,1,0:T(8,128)(2,1)S(1)}, bf16[32,8,640]{2,1,0:T(8,128)(2,1)S(1)}, u32[]{:S(2)}, u32[]{:S(2)}) collective-permute-start(bf16[32,8,640]{2,1,0:T(8,128)(2,1)S(1)} %all_to_all.21.mine_ref), channel_id=1, source_target_pairs={{0,12},{12,0},{24,36},{36,24},{48,60},{60,48},{72,84},{84,72},{96,... | collective-permute-start | bytes 983048 | tf_op jit(solution)/shard_map/ppermute | solution.py:310
  207.6 1.2 collective-permute-done.17.other_ref
  208.9 1.0 shard_map.109
  (21 shorter events, 0.3 us)
Async XLA Ops:
  0.6 1.0 copy-start
  1.6 18.0 %copy-start.5 = (s32[1,12,2]{1,2,0:T(2,128)S(1)}, s32[1,12,2]{1,2,0:T(2,128)}, u32[]{:S(2)}) copy-start(s32[1,12,2]{1,2,0:T(2,128)} %param.11) | copy-start | bytes 292
  1.6 18.2 %copy-start.1 = (bf16[1,12,256,256]{3,2,1,0:T(8,128)(2,1)S(1)}, bf16[1,12,256,256]{3,2,1,0:T(8,128)(2,1)}, u32[]{:S(2)}) copy-start(bf16[1,12,256,256]{3,2,1,0:T(8,128)(2,1)} %param.10) | copy-start | bytes 4718596
  3.5 35.3 %all-to-all-start = ((bf16[64,4,512]{2,1,0:T(4,128)(2,1)}), bf16[64,4,512]{2,1,0:T(4,128)(2,1)}, u32[]{:S(2)}, u32[]{:S(2)}) async-start(bf16[64,4,512]{2,1,0:T(4,128)(2,1)} %reshape.59), calls=%async_computation | async-start | bytes 524288 | tf_op jit(solution)/shard_map/all_to_all | solution.py:284
  23.0 23.3 %collective-permute-start.2 = (bf16[3,272,256]{2,1,0:T(8,128)(2,1)S(1)}, bf16[3,272,256]{2,1,0:T(8,128)(2,1)S(1)}, u32[]{:S(2)}, u32[]{:S(2)}) collective-permute-start(bf16[3,272,256]{2,1,0:T(8,128)(2,1)S(1)} %get-tuple-element.22), channel_id=1, source_target_pairs={{0,1},{1,0},{2,3},{3,2},{4,5},{5,4},{6,7},{7,6},{8,9},{9,8},{10,11... | collective-permute-start | bytes 1253384 | tf_op jit(solution)/shard_map/ppermute | solution.py:273
  33.8 12.6 %collective-permute-start.3 = (bf16[3,272,256]{2,1,0:T(8,128)(2,1)S(1)}, bf16[3,272,256]{2,1,0:T(8,128)(2,1)S(1)}, u32[]{:S(2)}, u32[]{:S(2)}) collective-permute-start(bf16[3,272,256]{2,1,0:T(8,128)(2,1)S(1)} %get-tuple-element.23), channel_id=1, source_target_pairs={{0,11},{1,2},{2,1},{3,4},{4,3},{5,6},{6,5},{7,8},{8,7},{9,10},{10,... | collective-permute-start | bytes 1253384 | tf_op jit(solution)/shard_map/ppermute | solution.py:273
  35.7 26.4 %collective-permute-start.4 = (bf16[3,272,256]{2,1,0:T(8,128)(2,1)S(1)}, bf16[3,272,256]{2,1,0:T(8,128)(2,1)S(1)}, u32[]{:S(2)}, u32[]{:S(2)}) collective-permute-start(bf16[3,272,256]{2,1,0:T(8,128)(2,1)S(1)} %get-tuple-element.24), channel_id=1, source_target_pairs={{0,2},{1,3},{2,0},{3,1},{4,6},{5,7},{6,4},{7,5},{8,10},{9,11},{10,... | collective-permute-start | bytes 1253384 | tf_op jit(solution)/shard_map/ppermute | solution.py:273
  39.8 22.2 %collective-permute-start.1 = (bf16[256,512]{1,0:T(8,128)(2,1)S(1)}, bf16[256,512]{1,0:T(8,128)(2,1)S(1)}, u32[]{:S(2)}, u32[]{:S(2)}) collective-permute-start(bf16[256,512]{1,0:T(8,128)(2,1)S(1)} %reshape.60.refs_4_), channel_id=1, source_target_pairs={{0,11},{1,2},{2,1},{3,4},{4,3},{5,6},{6,5},{7,8},{8,7},{9,10},{10,... | collective-permute-start | bytes 786440 | tf_op jit(solution)/shard_map/ppermute | solution.py:273
  42.0 20.0 %collective-permute-start = (bf16[256,512]{1,0:T(8,128)(2,1)S(1)}, bf16[256,512]{1,0:T(8,128)(2,1)S(1)}, u32[]{:S(2)}, u32[]{:S(2)}) collective-permute-start(bf16[256,512]{1,0:T(8,128)(2,1)S(1)} %reshape.60.refs_4_), channel_id=1, source_target_pairs={{0,1},{1,0},{2,3},{3,2},{4,5},{5,4},{6,7},{7,6},{8,9},{9,8},{10,11... | collective-permute-start | bytes 786440 | tf_op jit(solution)/shard_map/ppermute | solution.py:273
  62.1 71.3 %copy-start.2 = (bf16[512,512]{1,0:T(8,128)(2,1)S(1)}, bf16[512,512]{1,0:T(8,128)(2,1)}, u32[]{:S(2)}) copy-start(bf16[512,512]{1,0:T(8,128)(2,1)} %refs_3_.1) | copy-start | bytes 1572868
  62.1 71.3 %copy-start.3 = (bf16[256,512]{1,0:T(8,128)(2,1)S(1)}, bf16[256,512]{1,0:T(8,128)(2,1)}, u32[]{:S(2)}) copy-start(bf16[256,512]{1,0:T(8,128)(2,1)} %refs_5_.1) | copy-start | bytes 786436
  62.1 71.3 %copy-start.4 = (f32[512]{0:T(512)S(1)}, f32[512]{0:T(512)}, u32[]{:S(2)}) copy-start(f32[512]{0:T(512)} %param.14) | copy-start | bytes 6148
  62.1 9.6 %collective-permute-start.5 = (bf16[256,512]{1,0:T(8,128)(2,1)S(1)}, bf16[256,512]{1,0:T(8,128)(2,1)S(1)}, u32[]{:S(2)}, u32[]{:S(2)}) collective-permute-start(bf16[256,512]{1,0:T(8,128)(2,1)S(1)} %collective-permute-done.1.refs_15_), channel_id=1, source_target_pairs={{0,1},{1,0},{2,3},{3,2},{4,5},{5,4},{6,7},{7,6},{8,9},{9,8},{10,11... | collective-permute-start | bytes 786440 | tf_op jit(solution)/shard_map/ppermute | solution.py:273
  67.2 7.1 %collective-permute-start.6 = (bf16[256,512]{1,0:T(8,128)(2,1)S(1)}, bf16[256,512]{1,0:T(8,128)(2,1)S(1)}, u32[]{:S(2)}, u32[]{:S(2)}) collective-permute-start(bf16[256,512]{1,0:T(8,128)(2,1)S(1)} %collective-permute-done.refs_5_), channel_id=1, source_target_pairs={{0,11},{1,2},{2,1},{3,4},{4,3},{5,6},{6,5},{7,8},{8,7},{9,10},{10,... | collective-permute-start | bytes 786440 | tf_op jit(solution)/shard_map/ppermute | solution.py:273
  71.6 7.1 %collective-permute-start.8 = (bf16[256,512]{1,0:T(8,128)(2,1)S(1)}, bf16[256,512]{1,0:T(8,128)(2,1)S(1)}, u32[]{:S(2)}, u32[]{:S(2)}) collective-permute-start(bf16[256,512]{1,0:T(8,128)(2,1)S(1)} %collective-permute-done.5.refs_6_), channel_id=1, source_target_pairs={{0,11},{1,2},{2,1},{3,4},{4,3},{5,6},{6,5},{7,8},{8,7},{9,10},{10,... | collective-permute-start | bytes 786440 | tf_op jit(solution)/shard_map/ppermute | solution.py:273
  74.3 8.9 %collective-permute-start.7 = (bf16[256,512]{1,0:T(8,128)(2,1)S(1)}, bf16[256,512]{1,0:T(8,128)(2,1)S(1)}, u32[]{:S(2)}, u32[]{:S(2)}) collective-permute-start(bf16[256,512]{1,0:T(8,128)(2,1)S(1)} %collective-permute-done.6.refs_14_), channel_id=1, source_target_pairs={{0,1},{1,0},{2,3},{3,2},{4,5},{5,4},{6,7},{7,6},{8,9},{9,8},{10,11... | collective-permute-start | bytes 786440 | tf_op jit(solution)/shard_map/ppermute | solution.py:273
  78.7 8.3 %collective-permute-start.9 = (bf16[256,512]{1,0:T(8,128)(2,1)S(1)}, bf16[256,512]{1,0:T(8,128)(2,1)S(1)}, u32[]{:S(2)}, u32[]{:S(2)}) collective-permute-start(bf16[256,512]{1,0:T(8,128)(2,1)S(1)} %collective-permute-done.8.refs_13_), channel_id=1, source_target_pairs={{0,1},{1,0},{2,3},{3,2},{4,5},{5,4},{6,7},{7,6},{8,9},{9,8},{10,11... | collective-permute-start | bytes 786440 | tf_op jit(solution)/shard_map/ppermute | solution.py:273
  83.2 7.4 %collective-permute-start.10 = (bf16[256,512]{1,0:T(8,128)(2,1)S(1)}, bf16[256,512]{1,0:T(8,128)(2,1)S(1)}, u32[]{:S(2)}, u32[]{:S(2)}) collective-permute-start(bf16[256,512]{1,0:T(8,128)(2,1)S(1)} %collective-permute-done.7.refs_7_), channel_id=1, source_target_pairs={{0,11},{1,2},{2,1},{3,4},{4,3},{5,6},{6,5},{7,8},{8,7},{9,10},{10,... | collective-permute-start | bytes 786440 | tf_op jit(solution)/shard_map/ppermute | solution.py:273
  87.1 7.4 %collective-permute-start.12 = (bf16[256,512]{1,0:T(8,128)(2,1)S(1)}, bf16[256,512]{1,0:T(8,128)(2,1)S(1)}, u32[]{:S(2)}, u32[]{:S(2)}) collective-permute-start(bf16[256,512]{1,0:T(8,128)(2,1)S(1)} %collective-permute-done.9.refs_8_), channel_id=1, source_target_pairs={{0,11},{1,2},{2,1},{3,4},{4,3},{5,6},{6,5},{7,8},{8,7},{9,10},{10,... | collective-permute-start | bytes 786440 | tf_op jit(solution)/shard_map/ppermute | solution.py:273
  90.6 8.6 %collective-permute-start.11 = (bf16[256,512]{1,0:T(8,128)(2,1)S(1)}, bf16[256,512]{1,0:T(8,128)(2,1)S(1)}, u32[]{:S(2)}, u32[]{:S(2)}) collective-permute-start(bf16[256,512]{1,0:T(8,128)(2,1)S(1)} %collective-permute-done.10.refs_12_), channel_id=1, source_target_pairs={{0,1},{1,0},{2,3},{3,2},{4,5},{5,4},{6,7},{7,6},{8,9},{9,8},{10,11... | collective-permute-start | bytes 786440 | tf_op jit(solution)/shard_map/ppermute | solution.py:273
  94.5 8.3 %collective-permute-start.13 = (bf16[256,512]{1,0:T(8,128)(2,1)S(1)}, bf16[256,512]{1,0:T(8,128)(2,1)S(1)}, u32[]{:S(2)}, u32[]{:S(2)}) collective-permute-start(bf16[256,512]{1,0:T(8,128)(2,1)S(1)} %collective-permute-done.12.refs_11_), channel_id=1, source_target_pairs={{0,1},{1,0},{2,3},{3,2},{4,5},{5,4},{6,7},{7,6},{8,9},{9,8},{10,11... | collective-permute-start | bytes 786440 | tf_op jit(solution)/shard_map/ppermute | solution.py:273
  107.3 21.3 %collective-permute-start.14 = (bf16[256,512]{1,0:T(8,128)(2,1)S(1)}, bf16[256,512]{1,0:T(8,128)(2,1)S(1)}, u32[]{:S(2)}, u32[]{:S(2)}) collective-permute-start(bf16[256,512]{1,0:T(8,128)(2,1)S(1)} %get-tuple-element.32), channel_id=1, source_target_pairs={{0,4},{1,5},{2,6},{3,7},{4,8},{5,9},{6,10},{7,11},{8,0},{9,1},{10,... | collective-permute-start | bytes 786440 | tf_op jit(solution)/shard_map/ppermute | solution.py:273
  112.4 20.9 %collective-permute-start.15 = (bf16[256,512]{1,0:T(8,128)(2,1)S(1)}, bf16[256,512]{1,0:T(8,128)(2,1)S(1)}, u32[]{:S(2)}, u32[]{:S(2)}) collective-permute-start(bf16[256,512]{1,0:T(8,128)(2,1)S(1)} %get-tuple-element.33), channel_id=1, source_target_pairs={{0,8},{1,9},{2,10},{3,11},{4,0},{5,1},{6,2},{7,3},{8,4},{9,5},{10,... | collective-permute-start | bytes 786440 | tf_op jit(solution)/shard_map/ppermute | solution.py:273
  134.8 7.5 %collective-permute-start.16 = (bf16[256,640]{1,0:T(8,128)(2,1)S(1)}, bf16[256,640]{1,0:T(8,128)(2,1)S(1)}, u32[]{:S(2)}, u32[]{:S(2)}) collective-permute-start(bf16[256,640]{1,0:T(8,128)(2,1)S(1)} %get-tuple-element.36), channel_id=1, source_target_pairs={{0,12},{12,0},{24,36},{36,24},{48,60},{60,48},{72,84},{84,72},{96,... | collective-permute-start | bytes 983048 | tf_op jit(solution)/shard_map/ppermute | solution.py:304
  170.1 15.7 %all-to-all-start.2 = ((bf16[12,8,640]{2,1,0:T(8,128)(2,1)}), bf16[12,8,640]{2,1,0:T(8,128)(2,1)S(1)}, u32[]{:S(2)}, u32[]{:S(2)}) async-start(bf16[12,8,640]{2,1,0:T(8,128)(2,1)} %shard_map.107), calls=%async_computation.2 | async-start | bytes 245760 | tf_op jit(solution)/shard_map/all_to_all | solution.py:307
  201.1 7.7 %collective-permute-start.17 = (bf16[32,8,640]{2,1,0:T(8,128)(2,1)S(1)}, bf16[32,8,640]{2,1,0:T(8,128)(2,1)S(1)}, u32[]{:S(2)}, u32[]{:S(2)}) collective-permute-start(bf16[32,8,640]{2,1,0:T(8,128)(2,1)S(1)} %all_to_all.21.mine_ref), channel_id=1, source_target_pairs={{0,12},{12,0},{24,36},{36,24},{48,60},{60,48},{72,84},{84,72},{96,... | collective-permute-start | bytes 983048 | tf_op jit(solution)/shard_map/ppermute | solution.py:310

commit v4 on v3

--- a/solution.py
+++ b/solution.py
@@ -22,8 +22,8 @@
 
 def ring_place(place_ref, n):
     here, turn = place_ref[0], place_ref[1]
-    near = jnp.where(lax.rem(here, 2) == 0, 1, -1)
-    far = jnp.where(lax.rem(lax.div(lax.rem(here * turn + n, n), 2), 2) == 0, 1, -1)
+    near = jnp.where(lax.rem(here, 2) == 0, -1, 1)
+    far = jnp.where(lax.rem(lax.div(here, 2) + lax.div(1 - turn, 2), 2) == 0, turn, -turn)
     return here, turn, near, far
 
 
@@ -31,41 +31,43 @@
     return (0, near, -near, 2 * far)
 
 
+def own_slot(output, first, n):
+    return lax.rem(output - first + 3 * n, n)
+
+
 def bundle_tiles(place, count, coords, tile_set):
     n, rows, columns = tile_set.shape
-    size = n // STRIDE
+    size, groups = n // STRIDE, STRIDE - 1
 
     def kernel(place_ref, count_ref, coords_ref, tiles_ref, *refs):
-        out_refs, (meta, tile_sems, meta_sems) = refs[:STRIDE], refs[STRIDE:]
+        out_refs, (meta, tile_sems, meta_sems) = refs[:groups], refs[groups:]
         here, turn, near, far = ring_place(place_ref, n)
-        first = coords_ref[0]
         copies = []
-        for g, ahead in enumerate(routes(near, far)):
+        for g, ahead in enumerate(routes(near, far)[1:]):
             for p in range(size):
-                i = g * size + p
-                output = here + turn * (p * STRIDE + ahead)
-                slot = lax.rem(output - first + 3 * n, n)
+                slot = own_slot(here + turn * (p * STRIDE + ahead), coords_ref[0], n)
                 target = out_refs[g].at[p, pl.ds(0, rows)]
-                copies.append(pltpu.make_async_copy(tiles_ref.at[slot], target, tile_sems.at[i]))
+                sem = tile_sems.at[g * size + p]
+                copies.append(pltpu.make_async_copy(tiles_ref.at[slot], target, sem))
                 copies[-1].start()
                 block = jnp.where(slot < count_ref[0], coords_ref[2 * slot + 1], -1)
-                meta[i] = jnp.full(meta.shape[1:], block.astype(F32), F32).astype(BF16)
-                note = out_refs[g].at[p, pl.ds(rows, META_ROWS)]
-                copies.append(pltpu.make_async_copy(meta.at[i], note, meta_sems.at[i]))
-                copies[-1].start()
+                meta[g, p] = jnp.full(meta.shape[2:], block.astype(F32), F32).astype(BF16)
+            notes = out_refs[g].at[:, pl.ds(rows, META_ROWS)]
+            copies.append(pltpu.make_async_copy(meta.at[g], notes, meta_sems.at[g]))
+            copies[-1].start()
         for copy in copies:
             copy.wait()
 
     bundle = jax.ShapeDtypeStruct((size, rows + META_ROWS, columns), tile_set.dtype)
     return pl.pallas_call(
         kernel,
-        out_shape=[bundle] * STRIDE,
+        out_shape=[bundle] * groups,
         in_specs=[IN_SMEM] * 3 + [IN_PLACE],
-        out_specs=[IN_PLACE] * STRIDE,
+        out_specs=[IN_PLACE] * groups,
         scratch_shapes=[
-            pltpu.VMEM((n, META_ROWS, columns), tile_set.dtype),
-            pltpu.SemaphoreType.DMA((n,)),
-            pltpu.SemaphoreType.DMA((n,)),
+            pltpu.VMEM((groups, size, META_ROWS, columns), tile_set.dtype),
+            pltpu.SemaphoreType.DMA((groups * size,)),
+            pltpu.SemaphoreType.DMA((groups,)),
         ],
         compiler_params=PARAMS,
         cost_estimate=pl.CostEstimate(
@@ -74,56 +76,55 @@
     )(place, count, coords, tile_set)
 
 
-def partial_sums(place, bundles, blocks):
-    groups, size = len(bundles), bundles[0].shape[0]
-    n = len(blocks)
+def partial_sum(place, count, coords, tile_set, bundles, blocks, p):
+    groups, n = len(bundles), len(blocks)
     rows, width = blocks[0].shape
 
-    def kernel(place_ref, *refs):
-        bundle_refs = refs[:groups]
-        block_refs = refs[groups : groups + n]
-        out_refs = refs[groups + n : -2]
-        sums, which = refs[-2:]
+    def kernel(place_ref, count_ref, coords_ref, tiles_ref, *refs):
+        bundle_refs, block_refs = refs[:groups], refs[groups : groups + n]
+        out_ref, total, own, which, sem = refs[groups + n :]
         here, turn, near, _ = ring_place(place_ref, n)
+        slot = own_slot(here + turn * p * STRIDE, coords_ref[0], n)
+        fetch = pltpu.make_async_copy(tiles_ref.at[slot], own, sem)
+        fetch.start()
+
+        def away(block):
+            return jnp.where(block < 0, -1, lax.rem(near * turn * (block - here) + n, n))
+
+        which[0] = away(jnp.where(slot < count_ref[0], coords_ref[2 * slot + 1], -1))
         for g, bundle_ref in enumerate(bundle_refs):
-            for p in range(size):
-                note = bundle_ref[p, rows : rows + META_ROWS, :LANES].astype(F32)
-                block = jnp.max(note).astype(jnp.int32)
-                away = lax.rem(near * turn * (block - here) + n, n)
-                which[g * size + p] = jnp.where(block < 0, -1, away)
-        sums[...] = jnp.zeros_like(sums)
+            note = bundle_ref[p, rows : rows + META_ROWS, :LANES].astype(F32)
+            which[1 + g] = away(jnp.max(note).astype(jnp.int32))
+        total[...] = jnp.zeros_like(total)
+        fetch.wait()
         for d, block_ref in enumerate(block_refs):
-            for g, bundle_ref in enumerate(bundle_refs):
-
-                @pl.loop(0, size)
-                def _(p):
-                    @pl.when(which[g * size + p] == d)
-                    def _():
-                        sums[p] += jnp.dot(
-                            bundle_ref[p, :rows, :], block_ref[...], preferred_element_type=F32
-                        )
-
-        for p, out_ref in enumerate(out_refs):
-            out_ref[...] = sums[p].astype(out_ref.dtype)
-
-    return pl.pallas_call(
-        kernel,
-        out_shape=[
-            jax.ShapeDtypeStruct((rows, width), F32 if p == 0 else BF16) for p in range(size)
+            for g in range(groups + 1):
+
+                @pl.when(which[g] == d)
+                def _():
+                    tile = bundle_refs[g - 1][p, :rows, :] if g else own[...]
+                    total[...] += jnp.dot(tile, block_ref[...], preferred_element_type=F32)
+
+        out_ref[...] = total[...].astype(out_ref.dtype)
+
+    return pl.pallas_call(
+        kernel,
+        out_shape=jax.ShapeDtypeStruct((rows, width), BF16 if p else F32),
+        in_specs=[IN_SMEM] * 3 + [IN_PLACE] + [IN_VMEM] * (groups + n),
+        out_specs=IN_VMEM,
+        scratch_shapes=[
+            pltpu.VMEM((rows, width), F32),
+            pltpu.VMEM(tile_set.shape[1:], tile_set.dtype),
+            pltpu.SMEM((groups + 1,), jnp.int32),
+            pltpu.SemaphoreType.DMA,
         ],
-        in_specs=[IN_SMEM] + [IN_VMEM] * (groups + n),
-        out_specs=[IN_VMEM] * size,
-        scratch_shapes=[
-            pltpu.VMEM((size, rows, width), F32),
-            pltpu.SMEM((groups * size,), jnp.int32),
-        ],
         compiler_params=PARAMS,
         cost_estimate=pl.CostEstimate(
-            flops=2 * n * rows * rows * width,
-            bytes_accessed=6 * 1024 * 1024,
+            flops=2 * (groups + 1) * rows * rows * width,
+            bytes_accessed=4 * 1024 * 1024,
             transcendentals=0,
         ),
-    )(place, *bundles, *blocks)
+    )(place, count, coords, tile_set, *bundles, *blocks)
 
 
 def layer(core, sums, weight, bias, cotangent):
@@ -263,23 +264,27 @@
     slot_rows = block_rows // col_count
     exchange = functools.partial(lax.all_to_all, split_axis=0, concat_axis=0, tiled=True)
 
-    def permute(x, step):
+    def permute(x, ahead):
         pairs = []
         for col in range(col_count):
-            turn = 1 - 2 * (col % 2)
+            core = col % 2
             for row in range(row_count):
-                target = (row + turn * step(turn * row % row_count)) % row_count
+                target = (row + (1 - 2 * core) * ahead(core, row)) % row_count
                 pairs.append((col * row_count + row, col * row_count + target))
         return lax.ppermute(x, ("col", "row"), pairs)
 
-    def swap(x, side, reach=1):
-        return permute(x, lambda row: reach if row // reach % 2 == side else -reach)
+    def swap(x, side):
+        return permute(x, lambda core, row: 1 if row % 2 != side else -1)
+
+    def swap_far(x):
+        return permute(x, lambda core, row: -2 if (row // 2 + core) % 2 ^ core else 2)
 
     col, row = (lax.axis_index(axis).astype(jnp.int32) for axis in ("col", "row"))
     place = jnp.stack([row, 1 - 2 * lax.rem(col, 2)])
 
-    bundles = bundle_tiles(place, counts, coords.reshape(-1), tiles[0])
-    bundles = [bundles[0], swap(bundles[1], 0), swap(bundles[2], 1), swap(bundles[3], 0, 2)]
+    tile_list = (place, counts, coords.reshape(-1), tiles[0])
+    bundles = bundle_tiles(*tile_list)
+    bundles = [swap(bundles[0], 0), swap(bundles[1], 1), swap_far(bundles[2])]
     sent = features[pick[0]].reshape(col_count, slot_rows, width)
     blocked = exchange(sent, "col").reshape(block_rows, width)
 
@@ -293,8 +298,9 @@
         if behind is not None:
             blocks[row_count - step] = behind
 
-    sums = partial_sums(place, bundles, blocks)
-    sums = [sums[0]] + [permute(sums[p], lambda _, p=p: p * STRIDE) for p in range(1, len(sums))]
+    sums = [partial_sum(*tile_list, bundles, blocks, p) for p in range(row_count // STRIDE)]
+    for p in range(1, len(sums)):
+        sums[p] = permute(sums[p], lambda core, row, p=p: p * STRIDE)
     core = lax.rem(col, 2).reshape(1)
     hidden, keep, give = layer(core, sums, weight, bias.reshape(1, width), cotangent)
 

time: 211 us -> 202 us (0.957)
  blocking collectives: 42.4 us -> 36.4 us
  starting transfers between devices: 93.6 us -> 88.1 us
  waiting for transfers between devices: 57.2 us -> 60.1 us
    all_to_all x1, blocking collectives: 27.1 us -> 21.3 us  [on_device(): parts = exchange(parts, 'col', axis_index_groups=cores)]
    ppermute x1, starting transfers between devices: 6.22 us -> 2.46 us  [on_device(): parts = sum_two(keep, lax.ppermute(give, 'col', other_core))]
    ppermute x16, waiting for transfers between devices: 44.3 us -> 47.2 us  [permute(): return lax.ppermute(x, ('col', 'row'), pairs)]
    pallas_call x2 -> x4, Pallas kernels: 7.65 us -> 7.32 us  [the longest x3 5.63 us: partial_sum(): pl.pallas_call(kernel, out_shape=jax.ShapeDtypeStruct((rows, width), BF16...]
  transfers between devices with their start and end apart: 20 -> 20, of which waited for: 14 -> 15; matrix products, arithmetic and copies ran while one was open for 1% -> 1% of each run, Pallas kernels for 2% -> 3%
where the time goes in v4:
time: 202 us; the launch traced here: 201 us
  starting transfers between devices  88.1 us (44%)
  waiting for transfers between devices  60.1 us (30%)
  blocking collectives  36.4 us (18%)
  Pallas kernels  10.6 us (5%)
  local copies, waits for them, and re-layouts  3.37 us (2%)
    ppermute x16, starting transfers between devices, permute(): return lax.ppermute(x, ('col', 'row'), pairs)  60.1 us
    ppermute x16, waiting for transfers between devices, permute(): return lax.ppermute(x, ('col', 'row'), pairs)  47.2 us
    all_to_all x1, blocking collectives, on_device(): parts = exchange(parts, 'col', axis_index_groups=cores)  21.3 us
    all_to_all x1, starting transfers between devices, on_device(): blocked = exchange(sent, 'col').reshape(block_rows, width)  15.4 us
    all_to_all x1, blocking collectives, on_device(): mine = exchange(parts, 'col', axis_index_groups=cores)  15.1 us
    all_to_all x1, waiting for transfers between devices, on_device(): parts = exchange(sum_over_chips(parts, row_count), 'row')  10.4 us
    ppermute x1, starting transfers between devices, on_device(): other = lax.ppermute(mine, 'col', other_core)  6.47 us
    pallas_call x3, Pallas kernels, partial_sum(): pl.pallas_call(kernel, out_shape=jax.ShapeDtypeStruct((rows, width), BF16...  5.63 us
  transfers between devices with their start and end apart: 20, of which 15 were waited for; matrix products, arithmetic and copies ran while one was open for 1% of the time, Pallas kernels for 3%

profile of v4, /device:TPU:1, one launch (start us, length us, event | category | flops | bytes accessed | tf_op | source)
XLA Modules:
  0.0 201.0 jit_solution(4012353602709018784)
XLA Ops:
  0.6 0.7 compare_select_fusion
  1.6 1.2 gather_fusion
  2.8 0.8 reshape.60
  3.5 15.4 %all-to-all-start = ((bf16[64,4,512]{2,1,0:T(4,128)(2,1)}), bf16[64,4,512]{2,1,0:T(4,128)(2,1)}, u32[]{:S(2)}, u32[]{:S(2)}) async-start(bf16[64,4,512]{2,1,0:T(4,128)(2,1)} %reshape.60), calls=%async_computation | async-start | bytes 524288 | tf_op jit(solution)/shard_map/all_to_all | solution.py:289
  19.8 1.7 shard_map.103
  21.5 1.9 collective-permute-start.2
  23.4 11.0 %collective-permute-start.3 = (bf16[3,272,256]{2,1,0:T(8,128)(2,1)}, bf16[3,272,256]{2,1,0:T(8,128)(2,1)S(1)}, u32[]{:S(2)}, u32[]{:S(2)}) collective-permute-start(bf16[3,272,256]{2,1,0:T(8,128)(2,1)} %get-tuple-element.17), channel_id=1, source_target_pairs={{0,1},{1,0},{2,3},{3,2},{4,5},{5,4},{6,7},{7,6},{8,9},{9,8},{10,11... | collective-permute-start | bytes 1253384 | tf_op jit(solution)/shard_map/ppermute | solution.py:274
  34.5 2.8 %collective-permute-start.4 = (bf16[3,272,256]{2,1,0:T(8,128)(2,1)}, bf16[3,272,256]{2,1,0:T(8,128)(2,1)S(1)}, u32[]{:S(2)}, u32[]{:S(2)}) collective-permute-start(bf16[3,272,256]{2,1,0:T(8,128)(2,1)} %get-tuple-element.18), channel_id=1, source_target_pairs={{0,2},{1,3},{2,0},{3,1},{4,6},{5,7},{6,4},{7,5},{8,10},{9,11},{10,... | collective-permute-start | bytes 1253384 | tf_op jit(solution)/shard_map/ppermute | solution.py:274
  37.3 1.0 reshape.61.refs_3_
  38.3 5.4 %collective-permute-start.1 = (bf16[256,512]{1,0:T(8,128)(2,1)S(1)}, bf16[256,512]{1,0:T(8,128)(2,1)S(1)}, u32[]{:S(2)}, u32[]{:S(2)}) collective-permute-start(bf16[256,512]{1,0:T(8,128)(2,1)S(1)} %reshape.61.refs_3_), channel_id=1, source_target_pairs={{0,1},{1,0},{2,3},{3,2},{4,5},{5,4},{6,7},{7,6},{8,9},{9,8},{10,11... | collective-permute-start | bytes 786440 | tf_op jit(solution)/shard_map/ppermute | solution.py:274
  43.8 1.9 collective-permute-start
  45.7 9.1 %collective-permute-done.4.refs_2_ = bf16[3,272,256]{2,1,0:T(8,128)(2,1)S(1)} collective-permute-done((bf16[3,272,256]{2,1,0:T(8,128)(2,1)}, bf16[3,272,256]{2,1,0:T(8,128)(2,1)S(1)}, u32[]{:S(2)}, u32[]{:S(2)}) %collective-permute-start.4) | collective-permute-done | bytes 417824 | tf_op jit(solution)/shard_map/ppermute | solution.py:274
  54.8 2.9 %collective-permute-done.1.refs_14_ = bf16[256,512]{1,0:T(8,128)(2,1)S(1)} collective-permute-done((bf16[256,512]{1,0:T(8,128)(2,1)S(1)}, bf16[256,512]{1,0:T(8,128)(2,1)S(1)}, u32[]{:S(2)}, u32[]{:S(2)}) %collective-permute-start.1) | collective-permute-done | bytes 262176 | tf_op jit(solution)/shard_map/ppermute | solution.py:274
  57.7 1.9 collective-permute-start.5
  59.6 4.9 %collective-permute-start.6 = (bf16[256,512]{1,0:T(8,128)(2,1)S(1)}, bf16[256,512]{1,0:T(8,128)(2,1)S(1)}, u32[]{:S(2)}, u32[]{:S(2)}) collective-permute-start(bf16[256,512]{1,0:T(8,128)(2,1)S(1)} %collective-permute-done.refs_4_), channel_id=1, source_target_pairs={{0,1},{1,0},{2,3},{3,2},{4,5},{5,4},{6,7},{7,6},{8,9},{9,8},{10,11... | collective-permute-start | bytes 786440 | tf_op jit(solution)/shard_map/ppermute | solution.py:274
  64.5 0.6 collective-permute-done.5.refs_5_
  65.1 5.7 %collective-permute-start.8 = (bf16[256,512]{1,0:T(8,128)(2,1)S(1)}, bf16[256,512]{1,0:T(8,128)(2,1)S(1)}, u32[]{:S(2)}, u32[]{:S(2)}) collective-permute-start(bf16[256,512]{1,0:T(8,128)(2,1)S(1)} %collective-permute-done.5.refs_5_), channel_id=1, source_target_pairs={{0,1},{1,0},{2,3},{3,2},{4,5},{5,4},{6,7},{7,6},{8,9},{9,8},{10,11... | collective-permute-start | bytes 786440 | tf_op jit(solution)/shard_map/ppermute | solution.py:274
  70.7 1.9 collective-permute-start.7
  72.7 1.8 collective-permute-done.8.refs_12_
  74.5 1.9 collective-permute-start.9
  76.4 1.8 collective-permute-done.7.refs_6_
  78.2 2.8 %collective-permute-start.10 = (bf16[256,512]{1,0:T(8,128)(2,1)S(1)}, bf16[256,512]{1,0:T(8,128)(2,1)S(1)}, u32[]{:S(2)}, u32[]{:S(2)}) collective-permute-start(bf16[256,512]{1,0:T(8,128)(2,1)S(1)} %collective-permute-done.7.refs_6_), channel_id=1, source_target_pairs={{0,1},{1,0},{2,3},{3,2},{4,5},{5,4},{6,7},{7,6},{8,9},{9,8},{10,11... | collective-permute-start | bytes 786440 | tf_op jit(solution)/shard_map/ppermute | solution.py:274
  81.0 0.9 collective-permute-done.9.refs_7_
  81.9 4.6 %collective-permute-start.12 = (bf16[256,512]{1,0:T(8,128)(2,1)S(1)}, bf16[256,512]{1,0:T(8,128)(2,1)S(1)}, u32[]{:S(2)}, u32[]{:S(2)}) collective-permute-start(bf16[256,512]{1,0:T(8,128)(2,1)S(1)} %collective-permute-done.9.refs_7_), channel_id=1, source_target_pairs={{0,1},{1,0},{2,3},{3,2},{4,5},{5,4},{6,7},{7,6},{8,9},{9,8},{10,11... | collective-permute-start | bytes 786440 | tf_op jit(solution)/shard_map/ppermute | solution.py:274
  86.5 0.6 collective-permute-done.10.refs_11_
  87.1 1.9 collective-permute-start.11
  89.0 1.2 collective-permute-done.12.refs_10_
  90.2 2.1 %collective-permute-start.13 = (bf16[256,512]{1,0:T(8,128)(2,1)S(1)}, bf16[256,512]{1,0:T(8,128)(2,1)S(1)}, u32[]{:S(2)}, u32[]{:S(2)}) collective-permute-start(bf16[256,512]{1,0:T(8,128)(2,1)S(1)} %collective-permute-done.12.refs_10_), channel_id=1, source_target_pairs={{0,11},{1,2},{2,1},{3,4},{4,3},{5,6},{6,5},{7,8},{8,7},{9,10},{10,... | collective-permute-start | bytes 786440 | tf_op jit(solution)/shard_map/ppermute | solution.py:274
  92.3 3.8 %collective-permute-done.11.refs_8_ = bf16[256,512]{1,0:T(8,128)(2,1)S(1)} collective-permute-done((bf16[256,512]{1,0:T(8,128)(2,1)S(1)}, bf16[256,512]{1,0:T(8,128)(2,1)S(1)}, u32[]{:S(2)}, u32[]{:S(2)}) %collective-permute-start.11) | collective-permute-done | bytes 262176 | tf_op jit(solution)/shard_map/ppermute | solution.py:274
  96.1 2.5 %collective-permute-done.13.refs_9_ = bf16[256,512]{1,0:T(8,128)(2,1)S(1)} collective-permute-done((bf16[256,512]{1,0:T(8,128)(2,1)S(1)}, bf16[256,512]{1,0:T(8,128)(2,1)S(1)}, u32[]{:S(2)}, u32[]{:S(2)}) %collective-permute-start.13) | collective-permute-done | bytes 262176 | tf_op jit(solution)/shard_map/ppermute | solution.py:274
  98.6 1.7 shard_map.105
  100.4 2.5 %collective-permute-start.14 = (bf16[256,512]{1,0:T(8,128)(2,1)S(1)}, bf16[256,512]{1,0:T(8,128)(2,1)S(1)}, u32[]{:S(2)}, u32[]{:S(2)}) collective-permute-start(bf16[256,512]{1,0:T(8,128)(2,1)S(1)} %shard_map.105), channel_id=1, source_target_pairs={{0,4},{1,5},{2,6},{3,7},{4,8},{5,9},{6,10},{7,11},{8,0},{9,1},{10,... | collective-permute-start | bytes 786440 | tf_op jit(solution)/shard_map/ppermute | solution.py:274
  102.9 2.1 %shard_map.106 = bf16[256,512]{1,0:T(8,128)(2,1)S(1)} custom-call(s32[2]{0:T(128)S(1)} %pad_add_fusion.place_ref, s32[1]{0:T(128)S(6)} %copy.13.count_ref, s32[24]{0:T(128)S(1)} %reshape.59.coords_ref, bf16[12,256,256]{2,1,0:T(8,128)(2,1)S(1)} %bitcast.13, bf16[3,272,256]{2,1,0:T(8,128)(2,1)S(1)} %collective-permute-done.2.refs_0_, ...), custom_call_target="tpu_custom_call" | custom-call | flops 268435456 | bytes 4194304 | tf_op jit(solution)/shard_map/pallas_call | solution.py:110
  105.1 6.8 %collective-permute-start.15 = (bf16[256,512]{1,0:T(8,128)(2,1)S(1)}, bf16[256,512]{1,0:T(8,128)(2,1)S(1)}, u32[]{:S(2)}, u32[]{:S(2)}) collective-permute-start(bf16[256,512]{1,0:T(8,128)(2,1)S(1)} %shard_map.106), channel_id=1, source_target_pairs={{0,8},{1,9},{2,10},{3,11},{4,0},{5,1},{6,2},{7,3},{8,4},{9,5},{10,... | collective-permute-start | bytes 786440 | tf_op jit(solution)/shard_map/ppermute | solution.py:274
  111.9 1.8 shard_map.104.refs_0_
  113.7 13.8 %collective-permute-done.14.refs_1_ = bf16[256,512]{1,0:T(8,128)(2,1)S(1)} collective-permute-done((bf16[256,512]{1,0:T(8,128)(2,1)S(1)}, bf16[256,512]{1,0:T(8,128)(2,1)S(1)}, u32[]{:S(2)}, u32[]{:S(2)}) %collective-permute-start.14) | collective-permute-done | bytes 262176 | tf_op jit(solution)/shard_map/ppermute | solution.py:274
  127.5 8.2 %collective-permute-done.15.refs_2_ = bf16[256,512]{1,0:T(8,128)(2,1)S(1)} collective-permute-done((bf16[256,512]{1,0:T(8,128)(2,1)S(1)}, bf16[256,512]{1,0:T(8,128)(2,1)S(1)}, u32[]{:S(2)}, u32[]{:S(2)}) %collective-permute-start.15) | collective-permute-done | bytes 262176 | tf_op jit(solution)/shard_map/ppermute | solution.py:274
  135.7 1.4 shard_map.107
  137.1 2.5 %collective-permute-start.16 = (bf16[256,640]{1,0:T(8,128)(2,1)S(1)}, bf16[256,640]{1,0:T(8,128)(2,1)S(1)}, u32[]{:S(2)}, u32[]{:S(2)}) collective-permute-start(bf16[256,640]{1,0:T(8,128)(2,1)S(1)} %get-tuple-element.26), channel_id=1, source_target_pairs={{0,12},{12,0},{24,36},{36,24},{48,60},{60,48},{72,84},{84,72},{96,... | collective-permute-start | bytes 983048 | tf_op jit(solution)/shard_map/ppermute | solution.py:310
  139.6 1.2 collective-permute-done.16.right_ref
  140.9 21.3 %all_to_all.20.parts_ref = bf16[32,8,640]{2,1,0:T(8,128)(2,1)S(1)} all-to-all(bf16[32,8,640]{2,1,0:T(8,128)(2,1)S(1)} %bitcast.15), channel_id=1, replica_groups={{0,24,48,72,96,120,144,168,192,216,240,264,288,312,336,360,384,408,432,..., dimensions={0} | all-to-all | bytes 655360 | tf_op jit(solution)/shard_map/all_to_all | solution.py:312
  162.2 0.7 shard_map.109
  162.9 3.7 %all-to-all-start.2 = ((bf16[12,8,640]{2,1,0:T(8,128)(2,1)}), bf16[12,8,640]{2,1,0:T(8,128)(2,1)S(1)}, u32[]{:S(2)}, u32[]{:S(2)}) async-start(bf16[12,8,640]{2,1,0:T(8,128)(2,1)} %shard_map.109), calls=%async_computation.2 | async-start | bytes 245760 | tf_op jit(solution)/shard_map/all_to_all | solution.py:313
  166.7 10.4 %all-to-all-done.2.parts_ref = bf16[12,8,640]{2,1,0:T(8,128)(2,1)S(1)} async-done(((bf16[12,8,640]{2,1,0:T(8,128)(2,1)}), bf16[12,8,640]{2,1,0:T(8,128)(2,1)S(1)}, u32[]{:S(2)}, u32[]{:S(2)}) %all-to-all-start.2) | async-done | bytes 122912 | tf_op jit(solution)/shard_map/all_to_all | solution.py:313
  177.1 15.1 %all_to_all.21.mine_ref = bf16[32,8,640]{2,1,0:T(8,128)(2,1)S(1)} all-to-all(bf16[32,8,640]{2,1,0:T(8,128)(2,1)S(1)} %shard_map.110), channel_id=1, replica_groups={{0,24,48,72,96,120,144,168,192,216,240,264,288,312,336,360,384,408,432,..., dimensions={0} | all-to-all | bytes 655360 | tf_op jit(solution)/shard_map/all_to_all | solution.py:315
  192.2 6.5 %collective-permute-start.17 = (bf16[32,8,640]{2,1,0:T(8,128)(2,1)S(1)}, bf16[32,8,640]{2,1,0:T(8,128)(2,1)S(1)}, u32[]{:S(2)}, u32[]{:S(2)}) collective-permute-start(bf16[32,8,640]{2,1,0:T(8,128)(2,1)S(1)} %all_to_all.21.mine_ref), channel_id=1, source_target_pairs={{0,12},{12,0},{24,36},{36,24},{48,60},{60,48},{72,84},{84,72},{96,... | collective-permute-start | bytes 983048 | tf_op jit(solution)/shard_map/ppermute | solution.py:316
  198.7 1.2 collective-permute-done.17.other_ref
  200.0 1.0 shard_map.111
  (23 shorter events, 0.7 us)
Async XLA Ops:
  0.6 1.0 copy-start
  1.6 18.0 %copy-start.5 = (s32[1,12,2]{1,2,0:T(2,128)S(1)}, s32[1,12,2]{1,2,0:T(2,128)}, u32[]{:S(2)}) copy-start(s32[1,12,2]{1,2,0:T(2,128)} %param.11) | copy-start | bytes 292
  1.6 18.2 %copy-start.1 = (bf16[1,12,256,256]{3,2,1,0:T(8,128)(2,1)S(1)}, bf16[1,12,256,256]{3,2,1,0:T(8,128)(2,1)}, u32[]{:S(2)}) copy-start(bf16[1,12,256,256]{3,2,1,0:T(8,128)(2,1)} %param.10) | copy-start | bytes 4718596
  3.5 33.8 %all-to-all-start = ((bf16[64,4,512]{2,1,0:T(4,128)(2,1)}), bf16[64,4,512]{2,1,0:T(4,128)(2,1)}, u32[]{:S(2)}, u32[]{:S(2)}) async-start(bf16[64,4,512]{2,1,0:T(4,128)(2,1)} %reshape.60), calls=%async_computation | async-start | bytes 524288 | tf_op jit(solution)/shard_map/all_to_all | solution.py:289
  21.5 24.2 %collective-permute-start.2 = (bf16[3,272,256]{2,1,0:T(8,128)(2,1)}, bf16[3,272,256]{2,1,0:T(8,128)(2,1)S(1)}, u32[]{:S(2)}, u32[]{:S(2)}) collective-permute-start(bf16[3,272,256]{2,1,0:T(8,128)(2,1)} %get-tuple-element.16), channel_id=1, source_target_pairs={{0,11},{1,2},{2,1},{3,4},{4,3},{5,6},{6,5},{7,8},{8,7},{9,10},{10,... | collective-permute-start | bytes 1253384 | tf_op jit(solution)/shard_map/ppermute | solution.py:274
  23.4 22.2 %collective-permute-start.3 = (bf16[3,272,256]{2,1,0:T(8,128)(2,1)}, bf16[3,272,256]{2,1,0:T(8,128)(2,1)S(1)}, u32[]{:S(2)}, u32[]{:S(2)}) collective-permute-start(bf16[3,272,256]{2,1,0:T(8,128)(2,1)} %get-tuple-element.17), channel_id=1, source_target_pairs={{0,1},{1,0},{2,3},{3,2},{4,5},{5,4},{6,7},{7,6},{8,9},{9,8},{10,11... | collective-permute-start | bytes 1253384 | tf_op jit(solution)/shard_map/ppermute | solution.py:274
  34.5 20.3 %collective-permute-start.4 = (bf16[3,272,256]{2,1,0:T(8,128)(2,1)}, bf16[3,272,256]{2,1,0:T(8,128)(2,1)S(1)}, u32[]{:S(2)}, u32[]{:S(2)}) collective-permute-start(bf16[3,272,256]{2,1,0:T(8,128)(2,1)} %get-tuple-element.18), channel_id=1, source_target_pairs={{0,2},{1,3},{2,0},{3,1},{4,6},{5,7},{6,4},{7,5},{8,10},{9,11},{10,... | collective-permute-start | bytes 1253384 | tf_op jit(solution)/shard_map/ppermute | solution.py:274
  38.3 19.3 %collective-permute-start.1 = (bf16[256,512]{1,0:T(8,128)(2,1)S(1)}, bf16[256,512]{1,0:T(8,128)(2,1)S(1)}, u32[]{:S(2)}, u32[]{:S(2)}) collective-permute-start(bf16[256,512]{1,0:T(8,128)(2,1)S(1)} %reshape.61.refs_3_), channel_id=1, source_target_pairs={{0,1},{1,0},{2,3},{3,2},{4,5},{5,4},{6,7},{7,6},{8,9},{9,8},{10,11... | collective-permute-start | bytes 786440 | tf_op jit(solution)/shard_map/ppermute | solution.py:274
  43.8 13.9 %collective-permute-start = (bf16[256,512]{1,0:T(8,128)(2,1)S(1)}, bf16[256,512]{1,0:T(8,128)(2,1)S(1)}, u32[]{:S(2)}, u32[]{:S(2)}) collective-permute-start(bf16[256,512]{1,0:T(8,128)(2,1)S(1)} %reshape.61.refs_3_), channel_id=1, source_target_pairs={{0,11},{1,2},{2,1},{3,4},{4,3},{5,6},{6,5},{7,8},{8,7},{9,10},{10,... | collective-permute-start | bytes 786440 | tf_op jit(solution)/shard_map/ppermute | solution.py:274
  57.7 7.4 %collective-permute-start.5 = (bf16[256,512]{1,0:T(8,128)(2,1)S(1)}, bf16[256,512]{1,0:T(8,128)(2,1)S(1)}, u32[]{:S(2)}, u32[]{:S(2)}) collective-permute-start(bf16[256,512]{1,0:T(8,128)(2,1)S(1)} %collective-permute-done.1.refs_14_), channel_id=1, source_target_pairs={{0,11},{1,2},{2,1},{3,4},{4,3},{5,6},{6,5},{7,8},{8,7},{9,10},{10,... | collective-permute-start | bytes 786440 | tf_op jit(solution)/shard_map/ppermute | solution.py:274
  59.6 11.1 %collective-permute-start.6 = (bf16[256,512]{1,0:T(8,128)(2,1)S(1)}, bf16[256,512]{1,0:T(8,128)(2,1)S(1)}, u32[]{:S(2)}, u32[]{:S(2)}) collective-permute-start(bf16[256,512]{1,0:T(8,128)(2,1)S(1)} %collective-permute-done.refs_4_), channel_id=1, source_target_pairs={{0,1},{1,0},{2,3},{3,2},{4,5},{5,4},{6,7},{7,6},{8,9},{9,8},{10,11... | collective-permute-start | bytes 786440 | tf_op jit(solution)/shard_map/ppermute | solution.py:274
  65.1 9.4 %collective-permute-start.8 = (bf16[256,512]{1,0:T(8,128)(2,1)S(1)}, bf16[256,512]{1,0:T(8,128)(2,1)S(1)}, u32[]{:S(2)}, u32[]{:S(2)}) collective-permute-start(bf16[256,512]{1,0:T(8,128)(2,1)S(1)} %collective-permute-done.5.refs_5_), channel_id=1, source_target_pairs={{0,1},{1,0},{2,3},{3,2},{4,5},{5,4},{6,7},{7,6},{8,9},{9,8},{10,11... | collective-permute-start | bytes 786440 | tf_op jit(solution)/shard_map/ppermute | solution.py:274
  70.7 7.4 %collective-permute-start.7 = (bf16[256,512]{1,0:T(8,128)(2,1)S(1)}, bf16[256,512]{1,0:T(8,128)(2,1)S(1)}, u32[]{:S(2)}, u32[]{:S(2)}) collective-permute-start(bf16[256,512]{1,0:T(8,128)(2,1)S(1)} %collective-permute-done.6.refs_13_), channel_id=1, source_target_pairs={{0,11},{1,2},{2,1},{3,4},{4,3},{5,6},{6,5},{7,8},{8,7},{9,10},{10,... | collective-permute-start | bytes 786440 | tf_op jit(solution)/shard_map/ppermute | solution.py:274
  74.5 7.4 %collective-permute-start.9 = (bf16[256,512]{1,0:T(8,128)(2,1)S(1)}, bf16[256,512]{1,0:T(8,128)(2,1)S(1)}, u32[]{:S(2)}, u32[]{:S(2)}) collective-permute-start(bf16[256,512]{1,0:T(8,128)(2,1)S(1)} %collective-permute-done.8.refs_12_), channel_id=1, source_target_pairs={{0,11},{1,2},{2,1},{3,4},{4,3},{5,6},{6,5},{7,8},{8,7},{9,10},{10,... | collective-permute-start | bytes 786440 | tf_op jit(solution)/shard_map/ppermute | solution.py:274
  78.2 8.9 %collective-permute-start.10 = (bf16[256,512]{1,0:T(8,128)(2,1)S(1)}, bf16[256,512]{1,0:T(8,128)(2,1)S(1)}, u32[]{:S(2)}, u32[]{:S(2)}) collective-permute-start(bf16[256,512]{1,0:T(8,128)(2,1)S(1)} %collective-permute-done.7.refs_6_), channel_id=1, source_target_pairs={{0,1},{1,0},{2,3},{3,2},{4,5},{5,4},{6,7},{7,6},{8,9},{9,8},{10,11... | collective-permute-start | bytes 786440 | tf_op jit(solution)/shard_map/ppermute | solution.py:274
  81.9 8.3 %collective-permute-start.12 = (bf16[256,512]{1,0:T(8,128)(2,1)S(1)}, bf16[256,512]{1,0:T(8,128)(2,1)S(1)}, u32[]{:S(2)}, u32[]{:S(2)}) collective-permute-start(bf16[256,512]{1,0:T(8,128)(2,1)S(1)} %collective-permute-done.9.refs_7_), channel_id=1, source_target_pairs={{0,1},{1,0},{2,3},{3,2},{4,5},{5,4},{6,7},{7,6},{8,9},{9,8},{10,11... | collective-permute-start | bytes 786440 | tf_op jit(solution)/shard_map/ppermute | solution.py:274
  87.1 9.1 %collective-permute-start.11 = (bf16[256,512]{1,0:T(8,128)(2,1)S(1)}, bf16[256,512]{1,0:T(8,128)(2,1)S(1)}, u32[]{:S(2)}, u32[]{:S(2)}) collective-permute-start(bf16[256,512]{1,0:T(8,128)(2,1)S(1)} %collective-permute-done.10.refs_11_), channel_id=1, source_target_pairs={{0,11},{1,2},{2,1},{3,4},{4,3},{5,6},{6,5},{7,8},{8,7},{9,10},{10,... | collective-permute-start | bytes 786440 | tf_op jit(solution)/shard_map/ppermute | solution.py:274
  90.2 8.4 %collective-permute-start.13 = (bf16[256,512]{1,0:T(8,128)(2,1)S(1)}, bf16[256,512]{1,0:T(8,128)(2,1)S(1)}, u32[]{:S(2)}, u32[]{:S(2)}) collective-permute-start(bf16[256,512]{1,0:T(8,128)(2,1)S(1)} %collective-permute-done.12.refs_10_), channel_id=1, source_target_pairs={{0,11},{1,2},{2,1},{3,4},{4,3},{5,6},{6,5},{7,8},{8,7},{9,10},{10,... | collective-permute-start | bytes 786440 | tf_op jit(solution)/shard_map/ppermute | solution.py:274
  100.4 27.1 %collective-permute-start.14 = (bf16[256,512]{1,0:T(8,128)(2,1)S(1)}, bf16[256,512]{1,0:T(8,128)(2,1)S(1)}, u32[]{:S(2)}, u32[]{:S(2)}) collective-permute-start(bf16[256,512]{1,0:T(8,128)(2,1)S(1)} %shard_map.105), channel_id=1, source_target_pairs={{0,4},{1,5},{2,6},{3,7},{4,8},{5,9},{6,10},{7,11},{8,0},{9,1},{10,... | collective-permute-start | bytes 786440 | tf_op jit(solution)/shard_map/ppermute | solution.py:274
  105.0 30.6 %copy-start.2 = (bf16[512,512]{1,0:T(8,128)(2,1)S(1)}, bf16[512,512]{1,0:T(8,128)(2,1)}, u32[]{:S(2)}) copy-start(bf16[512,512]{1,0:T(8,128)(2,1)} %refs_3_.1) | copy-start | bytes 1572868
  105.1 30.6 %copy-start.3 = (bf16[256,512]{1,0:T(8,128)(2,1)S(1)}, bf16[256,512]{1,0:T(8,128)(2,1)}, u32[]{:S(2)}) copy-start(bf16[256,512]{1,0:T(8,128)(2,1)} %refs_5_.1) | copy-start | bytes 786436
  105.1 30.6 %copy-start.4 = (f32[512]{0:T(512)S(1)}, f32[512]{0:T(512)}, u32[]{:S(2)}) copy-start(f32[512]{0:T(512)} %param.14) | copy-start | bytes 6148
  105.1 30.6 %collective-permute-start.15 = (bf16[256,512]{1,0:T(8,128)(2,1)S(1)}, bf16[256,512]{1,0:T(8,128)(2,1)S(1)}, u32[]{:S(2)}, u32[]{:S(2)}) collective-permute-start(bf16[256,512]{1,0:T(8,128)(2,1)S(1)} %shard_map.106), channel_id=1, source_target_pairs={{0,8},{1,9},{2,10},{3,11},{4,0},{5,1},{6,2},{7,3},{8,4},{9,5},{10,... | collective-permute-start | bytes 786440 | tf_op jit(solution)/shard_map/ppermute | solution.py:274
  137.1 3.7 %collective-permute-start.16 = (bf16[256,640]{1,0:T(8,128)(2,1)S(1)}, bf16[256,640]{1,0:T(8,128)(2,1)S(1)}, u32[]{:S(2)}, u32[]{:S(2)}) collective-permute-start(bf16[256,640]{1,0:T(8,128)(2,1)S(1)} %get-tuple-element.26), channel_id=1, source_target_pairs={{0,12},{12,0},{24,36},{36,24},{48,60},{60,48},{72,84},{84,72},{96,... | collective-permute-start | bytes 983048 | tf_op jit(solution)/shard_map/ppermute | solution.py:310
  162.9 14.2 %all-to-all-start.2 = ((bf16[12,8,640]{2,1,0:T(8,128)(2,1)}), bf16[12,8,640]{2,1,0:T(8,128)(2,1)S(1)}, u32[]{:S(2)}, u32[]{:S(2)}) async-start(bf16[12,8,640]{2,1,0:T(8,128)(2,1)} %shard_map.109), calls=%async_computation.2 | async-start | bytes 245760 | tf_op jit(solution)/shard_map/all_to_all | solution.py:313
  192.2 7.7 %collective-permute-start.17 = (bf16[32,8,640]{2,1,0:T(8,128)(2,1)S(1)}, bf16[32,8,640]{2,1,0:T(8,128)(2,1)S(1)}, u32[]{:S(2)}, u32[]{:S(2)}) collective-permute-start(bf16[32,8,640]{2,1,0:T(8,128)(2,1)S(1)} %all_to_all.21.mine_ref), channel_id=1, source_target_pairs={{0,12},{12,0},{24,36},{36,24},{48,60},{60,48},{72,84},{84,72},{96,... | collective-permute-start | bytes 983048 | tf_op jit(solution)/shard_map/ppermute | solution.py:316

commit v5 on v4

--- a/solution.py
+++ b/solution.py
@@ -127,13 +127,28 @@
     )(place, count, coords, tile_set, *bundles, *blocks)
 
 
+def gradient_half(low, left, grad_pre, out_ref):
+    rows, width = grad_pre.shape
+    half = width // 2
+    over_nodes = (((0,), (0,)), ((), ()))
+    mine = jnp.where(low, left[:, :half], left[:, half:])
+    out_ref[:, :width] = lax.dot_general(
+        mine, grad_pre, over_nodes, preferred_element_type=F32
+    ).astype(BF16)
+    mine = jnp.where(low, grad_pre[:, :half], grad_pre[:, half:])
+    ones = jnp.ones((rows, LANES), BF16)
+    out_ref[:, width:] = lax.dot_general(
+        mine, ones, over_nodes, preferred_element_type=F32
+    ).astype(BF16)
+
+
 def layer(core, sums, weight, bias, cotangent):
     rows, width = cotangent.shape
-    parts, half = len(sums), width // 2
+    parts = len(sums)
 
     def kernel(core_ref, *refs):
         sum_refs = refs[:parts]
-        weight_ref, bias_ref, cot_ref, hidden_ref, keep_ref, give_ref = refs[parts:]
+        weight_ref, bias_ref, cot_ref, hidden_ref, agg_ref, grad_ref, give_ref = refs[parts:]
         total = sum_refs[0][...].astype(F32)
         for sum_ref in sum_refs[1:]:
             total = total + sum_ref[...].astype(F32)
@@ -142,32 +157,41 @@
         sig = jax.nn.sigmoid(pre)
         hidden_ref[...] = (pre * sig).astype(BF16)
         grad_pre = (cot_ref[...].astype(F32) * sig * (1.0 + pre * (1.0 - sig))).astype(BF16)
-        over_nodes = (((0,), (0,)), ((), ()))
-        ones = jnp.ones((rows, LANES), BF16)
-        first = core_ref[0] == 0
-        for out_ref, low in ((keep_ref, first), (give_ref, jnp.logical_not(first))):
-            left = jnp.where(low, aggregated[:, :half], aggregated[:, half:])
-            out_ref[:, :width] = lax.dot_general(
-                left, grad_pre, over_nodes, preferred_element_type=F32
-            ).astype(BF16)
-            left = jnp.where(low, grad_pre[:, :half], grad_pre[:, half:])
-            out_ref[:, width:] = lax.dot_general(
-                left, ones, over_nodes, preferred_element_type=F32
-            ).astype(BF16)
-
-    gradient = jax.ShapeDtypeStruct((half, width + LANES), BF16)
-    return pl.pallas_call(
-        kernel,
-        out_shape=(jax.ShapeDtypeStruct((rows, width), BF16), gradient, gradient),
+        agg_ref[...] = aggregated
+        grad_ref[...] = grad_pre
+        gradient_half(core_ref[0] != 0, aggregated, grad_pre, give_ref)
+
+    nodes = jax.ShapeDtypeStruct((rows, width), BF16)
+    return pl.pallas_call(
+        kernel,
+        out_shape=(nodes, nodes, nodes, jax.ShapeDtypeStruct((width // 2, width + LANES), BF16)),
         in_specs=[IN_SMEM] + [IN_VMEM] * (parts + 3),
-        out_specs=(IN_VMEM, IN_VMEM, IN_VMEM),
+        out_specs=(IN_VMEM,) * 4,
         compiler_params=PARAMS,
         cost_estimate=pl.CostEstimate(
-            flops=4 * rows * width * width,
+            flops=3 * rows * width * width,
             bytes_accessed=3 * 1024 * 1024,
             transcendentals=rows * width,
         ),
     )(core, *sums, weight, bias, cotangent)
+
+
+def own_half(core, aggregated, grad_pre):
+    rows, width = grad_pre.shape
+
+    def kernel(core_ref, agg_ref, grad_ref, keep_ref):
+        gradient_half(core_ref[0] == 0, agg_ref[...], grad_ref[...], keep_ref)
+
+    return pl.pallas_call(
+        kernel,
+        out_shape=jax.ShapeDtypeStruct((width // 2, width + LANES), BF16),
+        in_specs=[IN_SMEM, IN_VMEM, IN_VMEM],
+        out_specs=IN_VMEM,
+        compiler_params=PARAMS,
+        cost_estimate=pl.CostEstimate(
+            flops=rows * width * width, bytes_accessed=1024 * 1024, transcendentals=0
+        ),
+    )(core, aggregated, grad_pre)
 
 
 def sum_two(left, right):
@@ -302,7 +326,10 @@
     for p in range(1, len(sums)):
         sums[p] = permute(sums[p], lambda core, row, p=p: p * STRIDE)
     core = lax.rem(col, 2).reshape(1)
-    hidden, keep, give = layer(core, sums, weight, bias.reshape(1, width), cotangent)
+    hidden, aggregated, grad_pre, give = layer(
+        core, sums, weight, bias.reshape(1, width), cotangent
+    )
+    keep = own_half(core, aggregated, grad_pre)
 
     chips = col_count // 2
     cores = [[2 * chip + k for chip in range(chips)] for k in range(2)]

time: 202 us -> 202 us (level)
  no operation moved by 1% of the time
where the time goes in v5:
time: 202 us; the launch traced here: 201 us
  starting transfers between devices  88.8 us (44%)
  waiting for transfers between devices  60 us (30%)
  blocking collectives  36.9 us (18%)
  Pallas kernels  9.96 us (5%)
  local copies, waits for them, and re-layouts  3.37 us (2%)
    ppermute x16, starting transfers between devices, permute(): return lax.ppermute(x, ('col', 'row'), pairs)  60.1 us
    ppermute x16, waiting for transfers between devices, permute(): return lax.ppermute(x, ('col', 'row'), pairs)  47.4 us
    all_to_all x1, blocking collectives, on_device(): parts = exchange(parts, 'col', axis_index_groups=cores)  21.6 us
    all_to_all x1, starting transfers between devices, on_device(): blocked = exchange(sent, 'col').reshape(block_rows, width)  15.4 us
    all_to_all x1, blocking collectives, on_device(): mine = exchange(parts, 'col', axis_index_groups=cores)  15.3 us
    all_to_all x1, waiting for transfers between devices, on_device(): parts = exchange(sum_over_chips(parts, row_count), 'row')  10.4 us
    ppermute x1, starting transfers between devices, on_device(): other = lax.ppermute(mine, 'col', other_core)  6.49 us
    pallas_call x3, Pallas kernels, partial_sum(): pl.pallas_call(kernel, out_shape=jax.ShapeDtypeStruct((rows, width), BF16...  4.96 us
  transfers between devices with their start and end apart: 20, of which 15 were waited for; matrix products, arithmetic and copies ran while one was open for 1% of the time, Pallas kernels for 3%

profile of v5, /device:TPU:1, one launch (start us, length us, event | category | flops | bytes accessed | tf_op | source)
XLA Modules:
  0.0 201.4 jit_solution(2490849362816243182)
XLA Ops:
  0.6 0.7 compare_select_fusion
  1.6 1.2 gather_fusion
  2.8 0.8 reshape.60
  3.5 15.4 %all-to-all-start = ((bf16[64,4,512]{2,1,0:T(4,128)(2,1)}), bf16[64,4,512]{2,1,0:T(4,128)(2,1)}, u32[]{:S(2)}, u32[]{:S(2)}) async-start(bf16[64,4,512]{2,1,0:T(4,128)(2,1)} %reshape.60), calls=%async_computation | async-start | bytes 524288 | tf_op jit(solution)/shard_map/all_to_all | solution.py:313
  19.8 1.7 shard_map.103
  21.5 1.9 collective-permute-start.2
  23.4 11.0 %collective-permute-start.3 = (bf16[3,272,256]{2,1,0:T(8,128)(2,1)}, bf16[3,272,256]{2,1,0:T(8,128)(2,1)S(1)}, u32[]{:S(2)}, u32[]{:S(2)}) collective-permute-start(bf16[3,272,256]{2,1,0:T(8,128)(2,1)} %get-tuple-element.18), channel_id=1, source_target_pairs={{0,1},{1,0},{2,3},{3,2},{4,5},{5,4},{6,7},{7,6},{8,9},{9,8},{10,11... | collective-permute-start | bytes 1253384 | tf_op jit(solution)/shard_map/ppermute | solution.py:298
  34.5 2.8 %collective-permute-start.4 = (bf16[3,272,256]{2,1,0:T(8,128)(2,1)}, bf16[3,272,256]{2,1,0:T(8,128)(2,1)S(1)}, u32[]{:S(2)}, u32[]{:S(2)}) collective-permute-start(bf16[3,272,256]{2,1,0:T(8,128)(2,1)} %get-tuple-element.19), channel_id=1, source_target_pairs={{0,2},{1,3},{2,0},{3,1},{4,6},{5,7},{6,4},{7,5},{8,10},{9,11},{10,... | collective-permute-start | bytes 1253384 | tf_op jit(solution)/shard_map/ppermute | solution.py:298
  37.3 1.0 reshape.61.refs_3_
  38.3 5.4 %collective-permute-start.1 = (bf16[256,512]{1,0:T(8,128)(2,1)S(1)}, bf16[256,512]{1,0:T(8,128)(2,1)S(1)}, u32[]{:S(2)}, u32[]{:S(2)}) collective-permute-start(bf16[256,512]{1,0:T(8,128)(2,1)S(1)} %reshape.61.refs_3_), channel_id=1, source_target_pairs={{0,1},{1,0},{2,3},{3,2},{4,5},{5,4},{6,7},{7,6},{8,9},{9,8},{10,11... | collective-permute-start | bytes 786440 | tf_op jit(solution)/shard_map/ppermute | solution.py:298
  43.8 1.9 collective-permute-start
  45.7 9.1 %collective-permute-done.4.refs_2_ = bf16[3,272,256]{2,1,0:T(8,128)(2,1)S(1)} collective-permute-done((bf16[3,272,256]{2,1,0:T(8,128)(2,1)}, bf16[3,272,256]{2,1,0:T(8,128)(2,1)S(1)}, u32[]{:S(2)}, u32[]{:S(2)}) %collective-permute-start.4) | collective-permute-done | bytes 417824 | tf_op jit(solution)/shard_map/ppermute | solution.py:298
  54.8 2.9 %collective-permute-done.1.refs_14_ = bf16[256,512]{1,0:T(8,128)(2,1)S(1)} collective-permute-done((bf16[256,512]{1,0:T(8,128)(2,1)S(1)}, bf16[256,512]{1,0:T(8,128)(2,1)S(1)}, u32[]{:S(2)}, u32[]{:S(2)}) %collective-permute-start.1) | collective-permute-done | bytes 262176 | tf_op jit(solution)/shard_map/ppermute | solution.py:298
  57.7 1.9 collective-permute-start.5
  59.6 4.9 %collective-permute-start.6 = (bf16[256,512]{1,0:T(8,128)(2,1)S(1)}, bf16[256,512]{1,0:T(8,128)(2,1)S(1)}, u32[]{:S(2)}, u32[]{:S(2)}) collective-permute-start(bf16[256,512]{1,0:T(8,128)(2,1)S(1)} %collective-permute-done.refs_4_), channel_id=1, source_target_pairs={{0,1},{1,0},{2,3},{3,2},{4,5},{5,4},{6,7},{7,6},{8,9},{9,8},{10,11... | collective-permute-start | bytes 786440 | tf_op jit(solution)/shard_map/ppermute | solution.py:298
  64.5 0.6 collective-permute-done.5.refs_5_
  65.1 5.7 %collective-permute-start.8 = (bf16[256,512]{1,0:T(8,128)(2,1)S(1)}, bf16[256,512]{1,0:T(8,128)(2,1)S(1)}, u32[]{:S(2)}, u32[]{:S(2)}) collective-permute-start(bf16[256,512]{1,0:T(8,128)(2,1)S(1)} %collective-permute-done.5.refs_5_), channel_id=1, source_target_pairs={{0,1},{1,0},{2,3},{3,2},{4,5},{5,4},{6,7},{7,6},{8,9},{9,8},{10,11... | collective-permute-start | bytes 786440 | tf_op jit(solution)/shard_map/ppermute | solution.py:298
  70.7 1.9 collective-permute-start.7
  72.7 1.8 collective-permute-done.8.refs_12_
  74.5 1.9 collective-permute-start.9
  76.4 1.8 collective-permute-done.7.refs_6_
  78.2 2.8 %collective-permute-start.10 = (bf16[256,512]{1,0:T(8,128)(2,1)S(1)}, bf16[256,512]{1,0:T(8,128)(2,1)S(1)}, u32[]{:S(2)}, u32[]{:S(2)}) collective-permute-start(bf16[256,512]{1,0:T(8,128)(2,1)S(1)} %collective-permute-done.7.refs_6_), channel_id=1, source_target_pairs={{0,1},{1,0},{2,3},{3,2},{4,5},{5,4},{6,7},{7,6},{8,9},{9,8},{10,11... | collective-permute-start | bytes 786440 | tf_op jit(solution)/shard_map/ppermute | solution.py:298
  81.0 0.9 collective-permute-done.9.refs_7_
  81.9 4.6 %collective-permute-start.12 = (bf16[256,512]{1,0:T(8,128)(2,1)S(1)}, bf16[256,512]{1,0:T(8,128)(2,1)S(1)}, u32[]{:S(2)}, u32[]{:S(2)}) collective-permute-start(bf16[256,512]{1,0:T(8,128)(2,1)S(1)} %collective-permute-done.9.refs_7_), channel_id=1, source_target_pairs={{0,1},{1,0},{2,3},{3,2},{4,5},{5,4},{6,7},{7,6},{8,9},{9,8},{10,11... | collective-permute-start | bytes 786440 | tf_op jit(solution)/shard_map/ppermute | solution.py:298
  86.5 0.6 collective-permute-done.10.refs_11_
  87.0 1.9 collective-permute-start.11
  89.0 1.2 collective-permute-done.12.refs_10_
  90.2 2.1 %collective-permute-start.13 = (bf16[256,512]{1,0:T(8,128)(2,1)S(1)}, bf16[256,512]{1,0:T(8,128)(2,1)S(1)}, u32[]{:S(2)}, u32[]{:S(2)}) collective-permute-start(bf16[256,512]{1,0:T(8,128)(2,1)S(1)} %collective-permute-done.12.refs_10_), channel_id=1, source_target_pairs={{0,11},{1,2},{2,1},{3,4},{4,3},{5,6},{6,5},{7,8},{8,7},{9,10},{10,... | collective-permute-start | bytes 786440 | tf_op jit(solution)/shard_map/ppermute | solution.py:298
  92.3 3.8 %collective-permute-done.11.refs_8_ = bf16[256,512]{1,0:T(8,128)(2,1)S(1)} collective-permute-done((bf16[256,512]{1,0:T(8,128)(2,1)S(1)}, bf16[256,512]{1,0:T(8,128)(2,1)S(1)}, u32[]{:S(2)}, u32[]{:S(2)}) %collective-permute-start.11) | collective-permute-done | bytes 262176 | tf_op jit(solution)/shard_map/ppermute | solution.py:298
  96.1 2.5 %collective-permute-done.13.refs_9_ = bf16[256,512]{1,0:T(8,128)(2,1)S(1)} collective-permute-done((bf16[256,512]{1,0:T(8,128)(2,1)S(1)}, bf16[256,512]{1,0:T(8,128)(2,1)S(1)}, u32[]{:S(2)}, u32[]{:S(2)}) %collective-permute-start.13) | collective-permute-done | bytes 262176 | tf_op jit(solution)/shard_map/ppermute | solution.py:298
  98.6 1.7 shard_map.105
  100.4 2.3 %collective-permute-start.14 = (bf16[256,512]{1,0:T(8,128)(2,1)S(1)}, bf16[256,512]{1,0:T(8,128)(2,1)S(1)}, u32[]{:S(2)}, u32[]{:S(2)}) collective-permute-start(bf16[256,512]{1,0:T(8,128)(2,1)S(1)} %shard_map.105), channel_id=1, source_target_pairs={{0,4},{1,5},{2,6},{3,7},{4,8},{5,9},{6,10},{7,11},{8,0},{9,1},{10,... | collective-permute-start | bytes 786440 | tf_op jit(solution)/shard_map/ppermute | solution.py:298
  102.7 1.9 shard_map.106
  104.6 7.0 %collective-permute-start.15 = (bf16[256,512]{1,0:T(8,128)(2,1)S(1)}, bf16[256,512]{1,0:T(8,128)(2,1)S(1)}, u32[]{:S(2)}, u32[]{:S(2)}) collective-permute-start(bf16[256,512]{1,0:T(8,128)(2,1)S(1)} %shard_map.106), channel_id=1, source_target_pairs={{0,8},{1,9},{2,10},{3,11},{4,0},{5,1},{6,2},{7,3},{8,4},{9,5},{10,... | collective-permute-start | bytes 786440 | tf_op jit(solution)/shard_map/ppermute | solution.py:298
  111.7 1.3 shard_map.104.refs_0_
  113.0 14.0 %collective-permute-done.14.refs_1_ = bf16[256,512]{1,0:T(8,128)(2,1)S(1)} collective-permute-done((bf16[256,512]{1,0:T(8,128)(2,1)S(1)}, bf16[256,512]{1,0:T(8,128)(2,1)S(1)}, u32[]{:S(2)}, u32[]{:S(2)}) %collective-permute-start.14) | collective-permute-done | bytes 262176 | tf_op jit(solution)/shard_map/ppermute | solution.py:298
  127.0 8.2 %collective-permute-done.15.refs_2_ = bf16[256,512]{1,0:T(8,128)(2,1)S(1)} collective-permute-done((bf16[256,512]{1,0:T(8,128)(2,1)S(1)}, bf16[256,512]{1,0:T(8,128)(2,1)S(1)}, u32[]{:S(2)}, u32[]{:S(2)}) %collective-permute-start.15) | collective-permute-done | bytes 262176 | tf_op jit(solution)/shard_map/ppermute | solution.py:298
  135.2 1.1 shard_map.107
  136.4 2.7 %collective-permute-start.16 = (bf16[256,640]{1,0:T(8,128)(2,1)S(1)}, bf16[256,640]{1,0:T(8,128)(2,1)S(1)}, u32[]{:S(2)}, u32[]{:S(2)}) collective-permute-start(bf16[256,640]{1,0:T(8,128)(2,1)S(1)} %get-tuple-element.28), channel_id=1, source_target_pairs={{0,12},{12,0},{24,36},{36,24},{48,60},{60,48},{72,84},{84,72},{96,... | collective-permute-start | bytes 983048 | tf_op jit(solution)/shard_map/ppermute | solution.py:337
  139.4 0.9 collective-permute-done.16.right_ref
  140.4 21.6 %all_to_all.20.parts_ref = bf16[32,8,640]{2,1,0:T(8,128)(2,1)S(1)} all-to-all(bf16[32,8,640]{2,1,0:T(8,128)(2,1)S(1)} %bitcast.15), channel_id=1, replica_groups={{0,24,48,72,96,120,144,168,192,216,240,264,288,312,336,360,384,408,432,..., dimensions={0} | all-to-all | bytes 655360 | tf_op jit(solution)/shard_map/all_to_all | solution.py:339
  162.0 0.7 shard_map.110
  162.8 4.1 %all-to-all-start.2 = ((bf16[12,8,640]{2,1,0:T(8,128)(2,1)}), bf16[12,8,640]{2,1,0:T(8,128)(2,1)S(1)}, u32[]{:S(2)}, u32[]{:S(2)}) async-start(bf16[12,8,640]{2,1,0:T(8,128)(2,1)} %shard_map.110), calls=%async_computation.2 | async-start | bytes 245760 | tf_op jit(solution)/shard_map/all_to_all | solution.py:340
  166.8 10.4 %all-to-all-done.2.parts_ref = bf16[12,8,640]{2,1,0:T(8,128)(2,1)S(1)} async-done(((bf16[12,8,640]{2,1,0:T(8,128)(2,1)}), bf16[12,8,640]{2,1,0:T(8,128)(2,1)S(1)}, u32[]{:S(2)}, u32[]{:S(2)}) %all-to-all-start.2) | async-done | bytes 122912 | tf_op jit(solution)/shard_map/all_to_all | solution.py:340
  177.3 15.3 %all_to_all.21.mine_ref = bf16[32,8,640]{2,1,0:T(8,128)(2,1)S(1)} all-to-all(bf16[32,8,640]{2,1,0:T(8,128)(2,1)S(1)} %shard_map.111), channel_id=1, replica_groups={{0,24,48,72,96,120,144,168,192,216,240,264,288,312,336,360,384,408,432,..., dimensions={0} | all-to-all | bytes 655360 | tf_op jit(solution)/shard_map/all_to_all | solution.py:342
  192.6 6.5 %collective-permute-start.17 = (bf16[32,8,640]{2,1,0:T(8,128)(2,1)S(1)}, bf16[32,8,640]{2,1,0:T(8,128)(2,1)S(1)}, u32[]{:S(2)}, u32[]{:S(2)}) collective-permute-start(bf16[32,8,640]{2,1,0:T(8,128)(2,1)S(1)} %all_to_all.21.mine_ref), channel_id=1, source_target_pairs={{0,12},{12,0},{24,36},{36,24},{48,60},{60,48},{72,84},{84,72},{96,... | collective-permute-start | bytes 983048 | tf_op jit(solution)/shard_map/ppermute | solution.py:343
  199.1 1.2 collective-permute-done.17.other_ref
  200.4 1.0 shard_map.112
  (24 shorter events, 1.0 us)
Async XLA Ops:
  0.6 1.0 copy-start
  1.6 18.0 %copy-start.5 = (s32[1,12,2]{1,2,0:T(2,128)S(1)}, s32[1,12,2]{1,2,0:T(2,128)}, u32[]{:S(2)}) copy-start(s32[1,12,2]{1,2,0:T(2,128)} %param.11) | copy-start | bytes 292
  1.6 18.2 %copy-start.1 = (bf16[1,12,256,256]{3,2,1,0:T(8,128)(2,1)S(1)}, bf16[1,12,256,256]{3,2,1,0:T(8,128)(2,1)}, u32[]{:S(2)}) copy-start(bf16[1,12,256,256]{3,2,1,0:T(8,128)(2,1)} %param.10) | copy-start | bytes 4718596
  3.5 33.8 %all-to-all-start = ((bf16[64,4,512]{2,1,0:T(4,128)(2,1)}), bf16[64,4,512]{2,1,0:T(4,128)(2,1)}, u32[]{:S(2)}, u32[]{:S(2)}) async-start(bf16[64,4,512]{2,1,0:T(4,128)(2,1)} %reshape.60), calls=%async_computation | async-start | bytes 524288 | tf_op jit(solution)/shard_map/all_to_all | solution.py:313
  21.5 24.2 %collective-permute-start.2 = (bf16[3,272,256]{2,1,0:T(8,128)(2,1)}, bf16[3,272,256]{2,1,0:T(8,128)(2,1)S(1)}, u32[]{:S(2)}, u32[]{:S(2)}) collective-permute-start(bf16[3,272,256]{2,1,0:T(8,128)(2,1)} %get-tuple-element.17), channel_id=1, source_target_pairs={{0,11},{1,2},{2,1},{3,4},{4,3},{5,6},{6,5},{7,8},{8,7},{9,10},{10,... | collective-permute-start | bytes 1253384 | tf_op jit(solution)/shard_map/ppermute | solution.py:298
  23.4 22.2 %collective-permute-start.3 = (bf16[3,272,256]{2,1,0:T(8,128)(2,1)}, bf16[3,272,256]{2,1,0:T(8,128)(2,1)S(1)}, u32[]{:S(2)}, u32[]{:S(2)}) collective-permute-start(bf16[3,272,256]{2,1,0:T(8,128)(2,1)} %get-tuple-element.18), channel_id=1, source_target_pairs={{0,1},{1,0},{2,3},{3,2},{4,5},{5,4},{6,7},{7,6},{8,9},{9,8},{10,11... | collective-permute-start | bytes 1253384 | tf_op jit(solution)/shard_map/ppermute | solution.py:298
  34.5 20.3 %collective-permute-start.4 = (bf16[3,272,256]{2,1,0:T(8,128)(2,1)}, bf16[3,272,256]{2,1,0:T(8,128)(2,1)S(1)}, u32[]{:S(2)}, u32[]{:S(2)}) collective-permute-start(bf16[3,272,256]{2,1,0:T(8,128)(2,1)} %get-tuple-element.19), channel_id=1, source_target_pairs={{0,2},{1,3},{2,0},{3,1},{4,6},{5,7},{6,4},{7,5},{8,10},{9,11},{10,... | collective-permute-start | bytes 1253384 | tf_op jit(solution)/shard_map/ppermute | solution.py:298
  38.3 19.3 %collective-permute-start.1 = (bf16[256,512]{1,0:T(8,128)(2,1)S(1)}, bf16[256,512]{1,0:T(8,128)(2,1)S(1)}, u32[]{:S(2)}, u32[]{:S(2)}) collective-permute-start(bf16[256,512]{1,0:T(8,128)(2,1)S(1)} %reshape.61.refs_3_), channel_id=1, source_target_pairs={{0,1},{1,0},{2,3},{3,2},{4,5},{5,4},{6,7},{7,6},{8,9},{9,8},{10,11... | collective-permute-start | bytes 786440 | tf_op jit(solution)/shard_map/ppermute | solution.py:298
  43.8 13.9 %collective-permute-start = (bf16[256,512]{1,0:T(8,128)(2,1)S(1)}, bf16[256,512]{1,0:T(8,128)(2,1)S(1)}, u32[]{:S(2)}, u32[]{:S(2)}) collective-permute-start(bf16[256,512]{1,0:T(8,128)(2,1)S(1)} %reshape.61.refs_3_), channel_id=1, source_target_pairs={{0,11},{1,2},{2,1},{3,4},{4,3},{5,6},{6,5},{7,8},{8,7},{9,10},{10,... | collective-permute-start | bytes 786440 | tf_op jit(solution)/shard_map/ppermute | solution.py:298
  57.7 7.4 %collective-permute-start.5 = (bf16[256,512]{1,0:T(8,128)(2,1)S(1)}, bf16[256,512]{1,0:T(8,128)(2,1)S(1)}, u32[]{:S(2)}, u32[]{:S(2)}) collective-permute-start(bf16[256,512]{1,0:T(8,128)(2,1)S(1)} %collective-permute-done.1.refs_14_), channel_id=1, source_target_pairs={{0,11},{1,2},{2,1},{3,4},{4,3},{5,6},{6,5},{7,8},{8,7},{9,10},{10,... | collective-permute-start | bytes 786440 | tf_op jit(solution)/shard_map/ppermute | solution.py:298
  59.6 11.1 %collective-permute-start.6 = (bf16[256,512]{1,0:T(8,128)(2,1)S(1)}, bf16[256,512]{1,0:T(8,128)(2,1)S(1)}, u32[]{:S(2)}, u32[]{:S(2)}) collective-permute-start(bf16[256,512]{1,0:T(8,128)(2,1)S(1)} %collective-permute-done.refs_4_), channel_id=1, source_target_pairs={{0,1},{1,0},{2,3},{3,2},{4,5},{5,4},{6,7},{7,6},{8,9},{9,8},{10,11... | collective-permute-start | bytes 786440 | tf_op jit(solution)/shard_map/ppermute | solution.py:298
  65.1 9.4 %collective-permute-start.8 = (bf16[256,512]{1,0:T(8,128)(2,1)S(1)}, bf16[256,512]{1,0:T(8,128)(2,1)S(1)}, u32[]{:S(2)}, u32[]{:S(2)}) collective-permute-start(bf16[256,512]{1,0:T(8,128)(2,1)S(1)} %collective-permute-done.5.refs_5_), channel_id=1, source_target_pairs={{0,1},{1,0},{2,3},{3,2},{4,5},{5,4},{6,7},{7,6},{8,9},{9,8},{10,11... | collective-permute-start | bytes 786440 | tf_op jit(solution)/shard_map/ppermute | solution.py:298
  70.7 7.4 %collective-permute-start.7 = (bf16[256,512]{1,0:T(8,128)(2,1)S(1)}, bf16[256,512]{1,0:T(8,128)(2,1)S(1)}, u32[]{:S(2)}, u32[]{:S(2)}) collective-permute-start(bf16[256,512]{1,0:T(8,128)(2,1)S(1)} %collective-permute-done.6.refs_13_), channel_id=1, source_target_pairs={{0,11},{1,2},{2,1},{3,4},{4,3},{5,6},{6,5},{7,8},{8,7},{9,10},{10,... | collective-permute-start | bytes 786440 | tf_op jit(solution)/shard_map/ppermute | solution.py:298
  74.5 7.4 %collective-permute-start.9 = (bf16[256,512]{1,0:T(8,128)(2,1)S(1)}, bf16[256,512]{1,0:T(8,128)(2,1)S(1)}, u32[]{:S(2)}, u32[]{:S(2)}) collective-permute-start(bf16[256,512]{1,0:T(8,128)(2,1)S(1)} %collective-permute-done.8.refs_12_), channel_id=1, source_target_pairs={{0,11},{1,2},{2,1},{3,4},{4,3},{5,6},{6,5},{7,8},{8,7},{9,10},{10,... | collective-permute-start | bytes 786440 | tf_op jit(solution)/shard_map/ppermute | solution.py:298
  78.2 8.9 %collective-permute-start.10 = (bf16[256,512]{1,0:T(8,128)(2,1)S(1)}, bf16[256,512]{1,0:T(8,128)(2,1)S(1)}, u32[]{:S(2)}, u32[]{:S(2)}) collective-permute-start(bf16[256,512]{1,0:T(8,128)(2,1)S(1)} %collective-permute-done.7.refs_6_), channel_id=1, source_target_pairs={{0,1},{1,0},{2,3},{3,2},{4,5},{5,4},{6,7},{7,6},{8,9},{9,8},{10,11... | collective-permute-start | bytes 786440 | tf_op jit(solution)/shard_map/ppermute | solution.py:298
  81.9 8.3 %collective-permute-start.12 = (bf16[256,512]{1,0:T(8,128)(2,1)S(1)}, bf16[256,512]{1,0:T(8,128)(2,1)S(1)}, u32[]{:S(2)}, u32[]{:S(2)}) collective-permute-start(bf16[256,512]{1,0:T(8,128)(2,1)S(1)} %collective-permute-done.9.refs_7_), channel_id=1, source_target_pairs={{0,1},{1,0},{2,3},{3,2},{4,5},{5,4},{6,7},{7,6},{8,9},{9,8},{10,11... | collective-permute-start | bytes 786440 | tf_op jit(solution)/shard_map/ppermute | solution.py:298
  87.0 9.1 %collective-permute-start.11 = (bf16[256,512]{1,0:T(8,128)(2,1)S(1)}, bf16[256,512]{1,0:T(8,128)(2,1)S(1)}, u32[]{:S(2)}, u32[]{:S(2)}) collective-permute-start(bf16[256,512]{1,0:T(8,128)(2,1)S(1)} %collective-permute-done.10.refs_11_), channel_id=1, source_target_pairs={{0,11},{1,2},{2,1},{3,4},{4,3},{5,6},{6,5},{7,8},{8,7},{9,10},{10,... | collective-permute-start | bytes 786440 | tf_op jit(solution)/shard_map/ppermute | solution.py:298
  90.2 8.4 %collective-permute-start.13 = (bf16[256,512]{1,0:T(8,128)(2,1)S(1)}, bf16[256,512]{1,0:T(8,128)(2,1)S(1)}, u32[]{:S(2)}, u32[]{:S(2)}) collective-permute-start(bf16[256,512]{1,0:T(8,128)(2,1)S(1)} %collective-permute-done.12.refs_10_), channel_id=1, source_target_pairs={{0,11},{1,2},{2,1},{3,4},{4,3},{5,6},{6,5},{7,8},{8,7},{9,10},{10,... | collective-permute-start | bytes 786440 | tf_op jit(solution)/shard_map/ppermute | solution.py:298
  100.4 26.7 %collective-permute-start.14 = (bf16[256,512]{1,0:T(8,128)(2,1)S(1)}, bf16[256,512]{1,0:T(8,128)(2,1)S(1)}, u32[]{:S(2)}, u32[]{:S(2)}) collective-permute-start(bf16[256,512]{1,0:T(8,128)(2,1)S(1)} %shard_map.105), channel_id=1, source_target_pairs={{0,4},{1,5},{2,6},{3,7},{4,8},{5,9},{6,10},{7,11},{8,0},{9,1},{10,... | collective-permute-start | bytes 786440 | tf_op jit(solution)/shard_map/ppermute | solution.py:298
  104.6 30.6 %copy-start.2 = (bf16[512,512]{1,0:T(8,128)(2,1)S(1)}, bf16[512,512]{1,0:T(8,128)(2,1)}, u32[]{:S(2)}) copy-start(bf16[512,512]{1,0:T(8,128)(2,1)} %refs_3_.1) | copy-start | bytes 1572868
  104.6 30.6 %copy-start.3 = (bf16[256,512]{1,0:T(8,128)(2,1)S(1)}, bf16[256,512]{1,0:T(8,128)(2,1)}, u32[]{:S(2)}) copy-start(bf16[256,512]{1,0:T(8,128)(2,1)} %refs_5_.1) | copy-start | bytes 786436
  104.6 30.6 %copy-start.4 = (f32[512]{0:T(512)S(1)}, f32[512]{0:T(512)}, u32[]{:S(2)}) copy-start(f32[512]{0:T(512)} %param.14) | copy-start | bytes 6148
  104.6 30.6 %collective-permute-start.15 = (bf16[256,512]{1,0:T(8,128)(2,1)S(1)}, bf16[256,512]{1,0:T(8,128)(2,1)S(1)}, u32[]{:S(2)}, u32[]{:S(2)}) collective-permute-start(bf16[256,512]{1,0:T(8,128)(2,1)S(1)} %shard_map.106), channel_id=1, source_target_pairs={{0,8},{1,9},{2,10},{3,11},{4,0},{5,1},{6,2},{7,3},{8,4},{9,5},{10,... | collective-permute-start | bytes 786440 | tf_op jit(solution)/shard_map/ppermute | solution.py:298
  136.4 4.0 %collective-permute-start.16 = (bf16[256,640]{1,0:T(8,128)(2,1)S(1)}, bf16[256,640]{1,0:T(8,128)(2,1)S(1)}, u32[]{:S(2)}, u32[]{:S(2)}) collective-permute-start(bf16[256,640]{1,0:T(8,128)(2,1)S(1)} %get-tuple-element.28), channel_id=1, source_target_pairs={{0,12},{12,0},{24,36},{36,24},{48,60},{60,48},{72,84},{84,72},{96,... | collective-permute-start | bytes 983048 | tf_op jit(solution)/shard_map/ppermute | solution.py:337
  162.8 14.5 %all-to-all-start.2 = ((bf16[12,8,640]{2,1,0:T(8,128)(2,1)}), bf16[12,8,640]{2,1,0:T(8,128)(2,1)S(1)}, u32[]{:S(2)}, u32[]{:S(2)}) async-start(bf16[12,8,640]{2,1,0:T(8,128)(2,1)} %shard_map.110), calls=%async_computation.2 | async-start | bytes 245760 | tf_op jit(solution)/shard_map/all_to_all | solution.py:340
  192.6 7.7 %collective-permute-start.17 = (bf16[32,8,640]{2,1,0:T(8,128)(2,1)S(1)}, bf16[32,8,640]{2,1,0:T(8,128)(2,1)S(1)}, u32[]{:S(2)}, u32[]{:S(2)}) collective-permute-start(bf16[32,8,640]{2,1,0:T(8,128)(2,1)S(1)} %all_to_all.21.mine_ref), channel_id=1, source_target_pairs={{0,12},{12,0},{24,36},{36,24},{48,60},{60,48},{72,84},{84,72},{96,... | collective-permute-start | bytes 983048 | tf_op jit(solution)/shard_map/ppermute | solution.py:343
